TPU v7x, 32 devices: a whole 2x2x4 slice. The times are simulated.
32 devices in a mesh: items: 8 (over z, y), blk: 4 (over x, core).
Axes of the slice: x: 2, y: 2, z: 4, core: 2. Of those that a mesh axis runs over, the one named last changes fastest.
Arguments:
- block_input: bfloat16 [64, 4, 128, 768], P('items', 'blk'), may hold values from -6 to 6
- block_cotangent: bfloat16 [64, 4, 128, 768], P('items', 'blk'), may hold values from -6 to 6
- task_counts: int32 [64], P('items'), may hold values from 1 to 128, as said below
- group_mask: int32 [64, 4, 4], P('items'), may hold values from 0 to 1, as said below
- weight_qkv: float32 [768, 2304], P('items'), may hold values from -0.21875 to 0.21875
- weight_out: float32 [768, 768], P('items'), may hold values from -1.75 to 1.75
- weight_up: float32 [768, 3072], P('items'), may hold values from -0.21875 to 0.21875
- weight_down: float32 [3072, 768], P('items'), may hold values from -0.109375 to 0.109375
- vectors: float32 [12, 768], P(None, 'items'), may hold values from -1.2 to 1.4
- first_qkv: float32 [768, 2304], P('items'), may hold values from -80 to 80
- first_out: float32 [768, 768], P('items'), may hold values from -12 to 12
- first_up: float32 [768, 3072], P('items'), may hold values from -40 to 40
- first_down: float32 [3072, 768], P('items'), may hold values from -80 to 80
- first_vectors: float32 [12, 768], P(None, 'items'), may hold values from -128 to 128
- second_qkv: float32 [768, 2304], P('items'), may hold values from 8192 to 131072
- second_out: float32 [768, 768], P('items'), may hold values from 163.84 to 2621.44
- second_up: float32 [768, 3072], P('items'), may hold values from 1638.4 to 26214.4
- second_down: float32 [3072, 768], P('items'), may hold values from 6553.6 to 104857.6
- second_vectors: float32 [12, 768], P(None, 'items'), may hold values from 16384 to 262144
Outputs:
- block_output: bfloat16 [64, 4, 128, 768], P('items', 'blk')
- input_grad: float32 [64, 4, 128, 768], P('items', 'blk')
- new_weight_qkv: float32 [768, 2304], P('items')
- new_weight_out: float32 [768, 768], P('items')
- new_weight_up: float32 [768, 3072], P('items')
- new_weight_down: float32 [3072, 768], P('items')
- new_vectors: float32 [12, 768], P(None, 'items')
- new_first_qkv: float32 [768, 2304], P('items')
- new_first_out: float32 [768, 768], P('items')
- new_first_up: float32 [768, 3072], P('items')
- new_first_down: float32 [3072, 768], P('items')
- new_first_vectors: float32 [12, 768], P(None, 'items')
- new_second_qkv: float32 [768, 2304], P('items')
- new_second_out: float32 [768, 768], P('items')
- new_second_up: float32 [768, 3072], P('items')
- new_second_down: float32 [3072, 768], P('items')
- new_second_vectors: float32 [12, 768], P(None, 'items')
Inputs may be any that keep to these rules, and one draw needn't show every extreme that they name: `task_counts`: among the 8 items of each index of items, one has exactly 128 valid task tokens. group_mask[item, q, k] is 1 for k = q and 0 for k > q; among the 8 items of each index of items, one has ones everywhere on and below the diagonal.
All inputs are finite; a program needn't handle non-finite values.
Results may differ from a plain program's by a relative error of at most 0.012.
The roundings to bfloat16 on the way count: a program that leaves them out, or rounds other values in their place, can miss the bound.
Values may be sent and summed in bfloat16 or wider, within the bound.
A program may use at most 256 MiB of HBM per device.

v0:
```python
import math

import jax
import jax.numpy as jnp
from jax import lax
from jax.sharding import PartitionSpec as P

D = 768
H = 12
HD = 64
FF = 3072
GROUPS = 4
STEP = 5


norm_eps = 1e-06
beta_one = 0.9
beta_two = 0.5
adam_eps = 1e-08
weight_decay = 0.1
rates = (0.1, 0.8, 0.1, 0.06, 1.0)
masked_value = -1e30


def from_behind(block, axis, distance):
    devices = range(lax.axis_size(axis))
    route = [(i - distance, i) for i in devices if i - distance in devices]
    return lax.ppermute(block, axis, route)


def layer_norm(values, gain, shift):
    mean = jnp.mean(values, -1, keepdims=True)
    centred = values - mean
    variance = jnp.mean(centred * centred, -1, keepdims=True)
    return centred * lax.rsqrt(variance + norm_eps) * gain + shift


def gelu_tanh(values):
    return jax.nn.gelu(values, approximate=True)


def adamw(weight, first, second, grad, rate, decay_rate):
    first_new = beta_one * first + (1.0 - beta_one) * grad
    second_new = beta_two * second + (1.0 - beta_two) * grad * grad
    first_hat = first_new / (1.0 - beta_one**STEP)
    second_hat = second_new / (1.0 - beta_two**STEP)
    weight_new = weight - rate * (
        first_hat / (jnp.sqrt(second_hat) + adam_eps) + decay_rate * weight
    )
    return (weight_new, first_new, second_new)


def by_blocks(values, count):
    return values.reshape((values.shape[0] // count, count) + values.shape[1:])


def scores_of(queries, keys, allowed):
    raw = jnp.einsum("ighd,ijhd->ihgj", queries, keys, preferred_element_type=jnp.float32) * 0.125
    return jnp.where(allowed[:, None, None, :], raw, masked_value)


def attend_block(block):
    queries, keys, values, allowed = block
    scores = scores_of(queries, keys, allowed)
    top = jnp.max(scores, -1, keepdims=True)
    raw_weights = jnp.where(allowed[:, None, None, :], jnp.exp(scores - top), 0.0)
    total = jnp.sum(raw_weights, -1, keepdims=True)
    probs = (raw_weights / total).astype(jnp.bfloat16)
    mixed = jnp.einsum("ihgj,ijhd->ighd", probs, values, preferred_element_type=jnp.float32)
    return (mixed.astype(jnp.bfloat16), top + jnp.log(total))


def attend_back(block):
    queries, keys, values, allowed, grad_mixed, log_total = block
    scores = scores_of(queries, keys, allowed)
    probs = jnp.where(allowed[:, None, None, :], jnp.exp(scores - log_total), 0.0)
    grad_probs = jnp.einsum(
        "ighd,ijhd->ihgj", grad_mixed, values, preferred_element_type=jnp.float32
    )
    inner = jnp.sum(probs * grad_probs, -1, keepdims=True)
    grad_scores = (probs * (grad_probs - inner)).astype(jnp.bfloat16)
    grad_queries = (
        jnp.einsum("ihgj,ijhd->ighd", grad_scores, keys, preferred_element_type=jnp.float32) * 0.125
    )
    grad_keys = (
        jnp.einsum("ihgj,ighd->ijhd", grad_scores, queries, preferred_element_type=jnp.float32)
        * 0.125
    )
    grad_values = jnp.einsum(
        "ihgj,ighd->ijhd",
        probs.astype(jnp.bfloat16),
        grad_mixed,
        preferred_element_type=jnp.float32,
    )
    return (grad_queries, grad_keys, grad_values)


def body(
    block_input,
    block_cotangent,
    task_counts,
    group_mask,
    weight_qkv,
    weight_out,
    weight_up,
    weight_down,
    vectors,
    first_qkv,
    first_out,
    first_up,
    first_down,
    first_vectors,
    second_qkv,
    second_out,
    second_up,
    second_down,
    second_vectors,
):
    bf = jnp.bfloat16
    f32 = jnp.float32
    full_qkv, full_out, full_up, full_down, full_vecs = (
        lax.all_gather(weight_qkv.astype(bf), "items", axis=0, tiled=True),
        lax.all_gather(weight_out.astype(bf), "items", axis=0, tiled=True),
        lax.all_gather(weight_up.astype(bf), "items", axis=0, tiled=True),
        lax.all_gather(weight_down.astype(bf), "items", axis=0, tiled=True),
        lax.all_gather(vectors.astype(bf), "items", axis=1, tiled=True),
    )
    vecs = full_vecs.astype(f32)
    here = lax.axis_index("blk")
    local_in, local_cot = (block_input, block_cotangent)
    items_here = local_in.shape[0]
    group_len = local_in.shape[2]
    rows = items_here * local_in.shape[1] * group_len
    span = GROUPS * group_len
    seq = local_in.reshape(rows, D).astype(f32)
    norm_one, norm_one_back = jax.vjp(layer_norm, seq, vecs[0], vecs[1])
    first_low = norm_one.astype(bf)
    proj_bias = jnp.concatenate([vecs[4], jnp.zeros((D,), f32), vecs[5]])
    proj = (jnp.dot(first_low, full_qkv, preferred_element_type=f32) + proj_bias).astype(bf)
    query = proj[:, :D].reshape(rows // group_len, group_len, H, HD)
    pairs = proj[:, D:]
    order = jnp.arange(GROUPS, dtype=jnp.int32)
    place = jnp.arange(group_len, dtype=jnp.int32)
    slots = [pairs]
    moving = pairs
    for hop in range(1, GROUPS):
        moving = from_behind(moving, "blk", 1)
        slots.append(moving)
    slot_stack = jnp.stack(slots)
    key_group = here - order
    own_row = jnp.sum(group_mask * (order == here).astype(jnp.int32)[None, :, None], axis=1)
    slot_pick = (order[None, :] == key_group[:, None]).astype(jnp.int32)
    slot_open = jnp.sum(own_row[:, None, :] * slot_pick[None], -1)
    slot_open = slot_open * (key_group <= here).astype(jnp.int32)[None]
    counted = (place[None, None, :] < task_counts[:, None, None]) | (key_group != 0)[None, :, None]
    allowed = ((slot_open[:, :, None] > 0) & counted).reshape(items_here, span)
    joined = (
        slot_stack.reshape(GROUPS, items_here, group_len, 2 * D)
        .transpose(1, 0, 2, 3)
        .reshape(items_here, span, 2 * D)
    )
    batch = query.shape[0]
    step_items = math.gcd(batch, 4)
    keys = joined[:, :, :D].reshape(batch, span, H, HD)
    values = joined[:, :, D:].reshape(batch, span, H, HD)
    blocked = (
        by_blocks(query, step_items),
        by_blocks(keys, step_items),
        by_blocks(values, step_items),
        by_blocks(allowed, step_items),
    )
    mixed_blocks, log_total = lax.map(attend_block, blocked)
    mixed = mixed_blocks.reshape(rows, D)
    second_in = seq + jnp.dot(mixed, full_out, preferred_element_type=f32) + vecs[6]
    norm_two, norm_two_back = jax.vjp(layer_norm, second_in, vecs[2], vecs[3])
    second_low = norm_two.astype(bf)
    hidden = jnp.dot(second_low, full_up, preferred_element_type=f32) + vecs[8:].reshape(FF)
    gelu_out, gelu_back = jax.vjp(gelu_tanh, hidden)
    gelu_low = gelu_out.astype(bf)
    output = second_in + jnp.dot(gelu_low, full_down, preferred_element_type=f32) + vecs[7]
    output_low = output.astype(bf).reshape(local_in.shape)
    grad_y = local_cot.reshape(rows, D)
    grad_y32 = grad_y.astype(f32)
    grad_down = jnp.einsum("rf,rd->fd", gelu_low, grad_y, preferred_element_type=f32)
    bias_down = jnp.sum(grad_y32, 0)
    grad_gelu = jnp.einsum("rd,fd->rf", grad_y, full_down, preferred_element_type=f32)
    grad_hidden = gelu_back(grad_gelu)[0].astype(bf)
    grad_up = jnp.einsum("rd,rf->df", second_low, grad_hidden, preferred_element_type=f32)
    bias_up = jnp.sum(grad_hidden.astype(f32), 0).reshape(FF // D, D)
    grad_norm_two = jnp.einsum("rf,df->rd", grad_hidden, full_up, preferred_element_type=f32)
    back_two, gain_two, shift_two = norm_two_back(grad_norm_two)
    grad_second_in = grad_y32 + back_two
    bias_out = jnp.sum(grad_second_in, 0)
    grad_branch = grad_second_in.astype(bf)
    grad_out = jnp.einsum("rd,re->de", mixed, grad_branch, preferred_element_type=f32)
    grad_mixed = jnp.einsum("re,de->rd", grad_branch, full_out, preferred_element_type=f32).astype(
        bf
    )
    back_blocks = blocked + (
        by_blocks(grad_mixed.reshape(batch, group_len, H, HD), step_items),
        log_total,
    )
    grad_queries, grad_keys, grad_values = lax.map(attend_back, back_blocks)
    slot_grads = jnp.concatenate(
        [
            grad_keys.reshape(items_here, GROUPS, group_len, D),
            grad_values.reshape(items_here, GROUPS, group_len, D),
        ],
        -1,
    )
    slot_grads = slot_grads.transpose(1, 0, 2, 3).reshape(GROUPS, rows, 2 * D)
    carried = slot_grads[GROUPS - 1]
    for hop in range(GROUPS - 2, -1, -1):
        carried = from_behind(carried, "blk", -1)
        carried = carried + slot_grads[hop]
    grad_proj = jnp.concatenate([grad_queries.reshape(rows, D).astype(bf), carried.astype(bf)], -1)
    grad_qkv = jnp.einsum("rd,re->de", first_low, grad_proj, preferred_element_type=f32)
    proj_sums = jnp.sum(grad_proj.astype(f32), 0)
    grad_norm_one = jnp.einsum("re,de->rd", grad_proj, full_qkv, preferred_element_type=f32)
    back_one, gain_one, shift_one = norm_one_back(grad_norm_one)
    local_grad = (grad_second_in + back_one).reshape(local_in.shape)
    grad_vecs = jnp.concatenate(
        [
            jnp.stack(
                [
                    gain_one,
                    shift_one,
                    gain_two,
                    shift_two,
                    proj_sums[:D],
                    proj_sums[2 * D :],
                    bias_out,
                    bias_down,
                ]
            ),
            bias_up,
        ],
        0,
    )
    masters = (weight_qkv, weight_out, weight_up, weight_down, vectors)
    firsts = (first_qkv, first_out, first_up, first_down, first_vectors)
    seconds = (second_qkv, second_out, second_up, second_down, second_vectors)
    decays = (weight_decay, weight_decay, weight_decay, weight_decay, 0.0)
    shares = (
        lax.psum_scatter(grad_qkv, "items", scatter_dimension=0, tiled=True),
        lax.psum_scatter(grad_out, "items", scatter_dimension=0, tiled=True),
        lax.psum_scatter(grad_up, "items", scatter_dimension=0, tiled=True),
        lax.psum_scatter(grad_down, "items", scatter_dimension=0, tiled=True),
        lax.psum_scatter(grad_vecs, "items", scatter_dimension=1, tiled=True),
    )
    shares = lax.psum((shares[0], shares[1], shares[2], shares[3], shares[4]), "blk")
    updated = [
        adamw(masters[n], firsts[n], seconds[n], shares[n], rates[n], decays[n]) for n in range(5)
    ]
    return (
        output_low,
        local_grad,
        updated[0][0],
        updated[1][0],
        updated[2][0],
        updated[3][0],
        updated[4][0],
        updated[0][1],
        updated[1][1],
        updated[2][1],
        updated[3][1],
        updated[4][1],
        updated[0][2],
        updated[1][2],
        updated[2][2],
        updated[3][2],
        updated[4][2],
    )


def solution(mesh):
    return jax.shard_map(
        body,
        mesh=mesh,
        in_specs=(
            P("items", "blk", None, None),
            P("items", "blk", None, None),
            P("items"),
            P("items", None, None),
            P("items", None),
            P("items", None),
            P("items", None),
            P("items", None),
            P(None, "items"),
            P("items", None),
            P("items", None),
            P("items", None),
            P("items", None),
            P(None, "items"),
            P("items", None),
            P("items", None),
            P("items", None),
            P("items", None),
            P(None, "items"),
        ),
        out_specs=(
            P("items", "blk", None, None),
            P("items", "blk", None, None),
            P("items", None),
            P("items", None),
            P("items", None),
            P("items", None),
            P(None, "items"),
            P("items", None),
            P("items", None),
            P("items", None),
            P("items", None),
            P(None, "items"),
            P("items", None),
            P("items", None),
            P("items", None),
            P("items", None),
            P(None, "items"),
        ),
        check_vma=False,
    )
```

profile of v0, /device:TPU:0, one launch (start us, length us, event | category | flops | bytes accessed | tf_op | source)
XLA Modules:
  0.0 1053.1 jit_solution(9021384052657850672)
XLA Ops:
  13.7 32.4 %all-gather = bf16[8,96,12]{1,2,0:T(8,128)(2,1)S(1)} all-gather(bf16[1,96,12]{1,2,0:T(8,128)(2,1)S(1)} %convert_bitcast_fusion), channel_id=1, replica_groups=mesh['items'=8,'blk'=4] {'items'}, dimensions={0}, use_global_device_ids=true | all-gather | bytes 20736 | tf_op jit(solution)/shard_map/all_gather | solution.py:126
  48.0 30.8 %all-gather.6.cloned.1.call-done = bf16[768,2304]{1,0:T(8,128)(2,1)} async-done(((bf16[96,2304]{1,0:T(8,128)(2,1)}), bf16[768,2304]{1,0:T(8,128)(2,1)}) %all-gather.6.cloned.1.call-update) | async-done | bytes 3538960 | tf_op jit(solution)/shard_map/all_gather | solution.py:122
  93.4 34.7 %collective-permute-start.1 = (bf16[1024,1536]{1,0:T(8,128)(2,1)S(1)}, bf16[1024,1536]{1,0:T(8,128)(2,1)}, u32[]{:S(2)}, u32[]{:S(2)}) collective-permute-start(bf16[1024,1536]{1,0:T(8,128)(2,1)S(1)} %collective-permute-done), channel_id=1, source_target_pairs={{0,1},{1,2},{2,3},{4,5},{5,6},{6,7},{8,9},{9,10},{10,11},{12,13},{... | collective-permute-start | bytes 9437192 | tf_op jit(solution)/shard_map/ppermute | solution.py:28
  131.8 34.8 %collective-permute-start.2 = (bf16[1024,1536]{1,0:T(8,128)(2,1)}, bf16[1024,1536]{1,0:T(8,128)(2,1)}, u32[]{:S(2)}, u32[]{:S(2)}) collective-permute-start(bf16[1024,1536]{1,0:T(8,128)(2,1)} %collective-permute-done.1), channel_id=1, source_target_pairs={{0,1},{1,2},{2,3},{4,5},{5,6},{6,7},{8,9},{9,10},{10,11},{12,13},{... | collective-permute-start | bytes 9437192 | tf_op jit(solution)/shard_map/ppermute | solution.py:28
  185.5 8.7 copy.133
  194.2 8.7 copy.130
  202.9 29.7 %while.26 = (s32[]{:T(128)}, bf16[2,4,128,12,64]{2,1,0,4,3:T(4,128)(2,1)}, f32[2,4,12,128,1]{3,2,1,4,0:T(8,128)S(1)}, bf16[2,4,512,12,64]{2,4,3,1,0:T(8,128)(2,1...) while((s32[]{:T(128)}, ...), condition=%wide.region_7.8_spmd, body=%wide.region_4.7_spmd.sunk | while | flops 849733632 | bytes 72600712 | solution.py:172
  242.2 11.2 %fusion.87 = f32[1024,3072]{1,0:T(8,128)} fusion(bf16[768,3072]{1,0:T(8,128)(2,1)} %all-gather.10.cloned.1.call-done, f32[1024,768]{1,0:T(8,128)} %copy-done.3, f32[768]{0:T(1024)S(1)} %copy-done.49, f32[768]{0:T(1024)S(1)} %copy-done.42, f32[1024]{0:T(1024)S(1)} %fusion.80, f32[1024]{0:T(1024)S(1)} %broadcast_multiply_fusion), kind=kOutput, calls=%fused_computation.168 | convolution fusion | flops 4835770368 | bytes 20461568 | tf_op jit(solution)/shard_map/dot_general | solution.py:177
  253.4 30.1 %all-gather.12.cloned.1.call-done = bf16[3072,768]{1,0:T(8,128)(2,1)} async-done(((bf16[384,768]{1,0:T(8,128)(2,1)}), bf16[3072,768]{1,0:T(8,128)(2,1)}) %all-gather.12.cloned.1.call-update) | async-done | bytes 4718608 | tf_op jit(solution)/shard_map/all_gather | solution.py:125
  283.5 16.2 %convert_reduce_fusion = (f32[3072]{0:T(1024)}, bf16[1024,3072]{1,0:T(8,128)(2,1)S(1)}) fusion(f32[1024,3072]{1,0:T(8,128)} %fusion.87, f32[3072]{0:T(1024)S(1)} %copy-done.55, bf16[1024,768]{1,0:T(8,128)(2,1)S(1)} %bitcast.233, bf16[3072,768]{1,0:T(8,128)(2,1)} %all-gather.12.cloned.1.call-done), kind=kOutput, calls=%fused_computation.66 | convolution fusion | flops 4904186880 | bytes 25190400 | tf_op jit(solution)/shard_map/rd,fd->rf/dot_general | solution.py:186
  299.7 10.8 %multiply_reduce_fusion.1 = (f32[768]{0:T(1024)}, f32[1024]{0:T(1024)S(1)}, f32[768]{0:T(1024)}, f32[1024,768]{1,0:T(8,128)S(1)}) fusion(f32[1024,768]{1,0:T(8,128)S(1)} %copy-done.4, f32[1024]{0:T(1024)S(1)} %fusion.80, f32[1024]{0:T(1024)S(1)} %broadcast_multiply_fusion, f32[768]{0:T(1024)S(1)} %copy-done.42, ...), kind=kOutput, calls=%fused_computation.94 | convolution fusion | flops 4838126592 | bytes 17323008 | tf_op jit(solution)/shard_map/rf,df->rd/dot_general | solution.py:190
  326.0 11.1 %fusion.86 = f32[768,3072]{1,0:T(8,128)} fusion(bf16[1024,3072]{1,0:T(8,128)(2,1)} %copy-done.13, f32[1024,768]{1,0:T(8,128)} %copy-done.3, f32[768]{0:T(1024)S(1)} %copy-done.49, f32[768]{0:T(1024)S(1)} %copy-done.42, f32[1024]{0:T(1024)S(1)} %fusion.80, f32[1024]{0:T(1024)S(1)} %broadcast_multiply_fusion), kind=kOutput, calls=%fused_computation.167 | convolution fusion | flops 4835770368 | bytes 18888704 | tf_op jit(solution)/shard_map/rd,rf->df/dot_general | solution.py:188
  337.2 66.1 %while.27 = (s32[]{:T(128)}, bf16[2,4,128,12,64]{2,4,3,1,0:T(8,128)(2,1)}, f32[2,4,512,12,64]{2,4,3,1,0:T(8,128)}, f32[2,4,512,12,64]{2,4,3,1,0:T(8,128)}, bf16[...) while((s32[]{:T(128)}, ...), condition=%wide.region_14.15_spmd, body=%wide.region_12.14_spmd.sunk | while | flops 2071848960 | bytes 135451856 | solution.py:203
  346.3 8.8 multiply_reduce_fusion.7
  379.2 8.8 multiply_reduce_fusion.7
  403.3 14.6 %reshape.291 = f32[8,4,128,768]{2,1,3,0:T(4,128)} reshape(f32[2,4,512,12,64]{2,4,3,1,0:T(8,128)} %get-tuple-element.113) | data formatting | bytes 25165824 | tf_op jit(solution)/shard_map/reshape | solution.py:207
  417.9 14.6 %reshape.290 = f32[8,4,128,768]{2,1,3,0:T(4,128)} reshape(f32[2,4,512,12,64]{2,4,3,1,0:T(8,128)} %get-tuple-element.112) | data formatting | bytes 25165824 | tf_op jit(solution)/shard_map/reshape | solution.py:206
  432.5 25.7 %maximum_bitcast_fusion = f32[4,8,128,1536]{2,0,3,1:T(4,128)} fusion(f32[8,4,128,768]{2,1,3,0:T(4,128)} %reshape.291, f32[8,4,128,768]{2,1,3,0:T(4,128)} %reshape.290), kind=kLoop, calls=%fused_computation.55 | loop fusion | flops 6291456 | bytes 50331648 | tf_op jit(solution)/shard_map/transpose | solution.py:211
  458.2 42.6 %fusion.97 = (f32[1,8,128,1536]{2,0,3,1:T(1,128)}, f32[1,8,128,1536]{2,0,3,1:T(1,128)}, f32[1,8,128,1536]{2,0,3,1:T(1,128)}, f32[1,8,128,1536]{2,0,3,1:T(1,128)}) fusion(f32[4,8,128,1536]{2,0,3,1:T(4,128)} %maximum_bitcast_fusion), kind=kLoop, calls=%fused_computation.173 | loop fusion | bytes 50331648 | tf_op jit(solution)/shard_map/slice | solution.py:215
  500.8 16.1 %copy.140 = f32[1,8,128,1536]{3,2,1,0:T(8,128)} copy(f32[1,8,128,1536]{2,0,3,1:T(1,128)} %get-tuple-element.397) | data formatting | bytes 12582912 | tf_op jit(solution)/shard_map/slice | solution.py:212
  518.2 13.0 %fusion.88 = f32[3072,768]{1,0:T(8,128)} fusion(bf16[1024,768]{1,0:T(8,128)(2,1)S(1)} %bitcast.234, f32[1024,3072]{1,0:T(8,128)} %fusion.87, f32[3072]{0:T(1024)S(1)} %copy-done.56), kind=kOutput, calls=%fused_computation.169 | convolution fusion | flops 4863295488 | bytes 23605248 | tf_op jit(solution)/shard_map/rf,rd->fd/dot_general | solution.py:184
  531.3 15.9 %copy.141 = f32[1,8,128,1536]{3,2,1,0:T(8,128)} copy(f32[1,8,128,1536]{2,0,3,1:T(1,128)} %get-tuple-element.396) | data formatting | bytes 12582912 | tf_op jit(solution)/shard_map/slice | solution.py:215
  547.2 8.7 bitcast_add_fusion.2
  557.2 16.0 %copy.142 = f32[1,8,128,1536]{3,2,1,0:T(8,128)} copy(f32[1,8,128,1536]{2,0,3,1:T(1,128)} %get-tuple-element.395) | data formatting | bytes 12582912 | tf_op jit(solution)/shard_map/slice | solution.py:215
  573.2 37.3 %collective-permute-done.4 = f32[1024,1536]{1,0:T(8,128)} collective-permute-done((f32[1024,1536]{1,0:T(8,128)}, f32[1024,1536]{1,0:T(8,128)}, u32[]{:S(2)}, u32[]{:S(2)}) %collective-permute-start.4) | collective-permute-done | bytes 6291488 | tf_op jit(solution)/shard_map/ppermute | solution.py:28
  610.4 8.7 bitcast_add_fusion.1
  624.0 16.1 %copy.143 = f32[1,8,128,1536]{3,2,1,0:T(8,128)} copy(f32[1,8,128,1536]{2,0,3,1:T(1,128)} %get-tuple-element.394) | data formatting | bytes 12582912 | tf_op jit(solution)/shard_map/slice | solution.py:215
  640.0 52.5 %collective-permute-done.5 = f32[1024,1536]{1,0:T(8,128)} collective-permute-done((f32[1024,1536]{1,0:T(8,128)}, f32[1024,1536]{1,0:T(8,128)}, u32[]{:S(2)}, u32[]{:S(2)}) %collective-permute-start.5) | collective-permute-done | bytes 6291488 | tf_op jit(solution)/shard_map/ppermute | solution.py:28
  720.3 172.3 %reduce-scatter.8.cloned.1.call-done = f32[96,2304]{1,0:T(8,128)} async-done(((f32[768,2304]{1,0:T(8,128)}), f32[96,2304]{1,0:T(8,128)}) %reduce-scatter.8.cloned.1.call-update) | async-done | bytes 884752 | tf_op jit(solution)/shard_map/reduce_scatter | solution.py:245
  892.6 13.6 %add_convert_fusion.1 = bf16[1024,768]{1,0:T(8,128)(2,1)} fusion(f32[1024,768]{1,0:T(8,128)} %copy-done.3, bf16[3072,768]{1,0:T(8,128)(2,1)} %all-gather.12.cloned.1.call-done, f32[768]{0:T(1024)S(1)} %copy-done.61, f32[1024,3072]{1,0:T(8,128)} %fusion.87, f32[3072]{0:T(1024)S(1)} %copy-done.56), kind=kOutput, calls=%fused_computation.98 | convolution fusion | flops 4865654784 | bytes 22035456 | tf_op jit(solution)/shard_map/dot_general | solution.py:180
  908.7 48.6 %reduce-scatter.16.cloned.1.call-done = f32[96,12]{1,0:T(8,128)} async-done(((f32[768,12]{1,0:T(8,128)}), f32[96,12]{1,0:T(8,128)}) %reduce-scatter.16.cloned.1.call-update) | async-done | bytes 4624
  964.7 69.6 %all-reduce.3.cloned.1.call-done = (f32[96,2304]{1,0:T(8,128)}, f32[96,768]{1,0:T(8,128)}, f32[96,3072]{1,0:T(8,128)}, f32[384,768]{1,0:T(8,128)}) async-done(((f32[96,2304]{1,0:T(8,128)}, f32[96,768]{1,0:T(8,128)}, f32[96,3072]{1,0:T(8,128)}, f32[384,768]{1,0:T(8,128)}), (f32[96,2304]{1,0:T(8,128)}, f32[96,768]{1,0:T(8,128)}, f32[96,3072]{1,0:T(8,128)}, f32[384,768]{1,0:T(8,128)})) %all-reduce.3.cloned.1.call-update) | async-done | bytes 3538960 | tf_op jit(solution)/shard_map/psum | solution.py:251
  (289 shorter events, 204.3 us)
Async XLA Ops:
  7.2 71.7 %all-gather.6.cloned.1.call-start = ((), (), s32[]{:S(2)}) async-start(), calls=%async_computation.5 | async-start | bytes 3981312 | tf_op jit(solution)/shard_map/all_gather | solution.py:122
  9.4 227.1 %all-gather.8.cloned.1.call-start = ((), (), s32[]{:S(2)}) async-start(), calls=%async_computation.6 | async-start | bytes 1327104 | tf_op jit(solution)/shard_map/all_gather | solution.py:123
  11.1 231.0 %all-gather.10.cloned.1.call-start = ((), (), s32[]{:S(2)}) async-start(), calls=%async_computation.7 | async-start | bytes 5308416 | tf_op jit(solution)/shard_map/all_gather | solution.py:124
  12.1 271.4 %all-gather.12.cloned.1.call-start = ((), (), s32[]{:S(2)}) async-start(), calls=%async_computation.8 | async-start | bytes 5308416 | tf_op jit(solution)/shard_map/all_gather | solution.py:125
  12.5 72.5 %copy-start.45 = (f32[1024]{0:T(1024)}, f32[1024]{0:T(1024)S(1)}, u32[]{:S(2)}) copy-start(f32[1024]{0:T(1024)S(1)} %get-tuple-element.402) | copy-start | bytes 12292
  13.7 71.3 %copy-start.47 = (f32[1024]{0:T(1024)}, f32[1024]{0:T(1024)S(1)}, u32[]{:S(2)}) copy-start(f32[1024]{0:T(1024)S(1)} %bitcast_rsqrt_fusion) | copy-start | bytes 12292
  85.0 81.7 %copy-start.23 = (f32[384,768]{1,0:T(8,128)S(1)}, f32[384,768]{1,0:T(8,128)}, u32[]{:S(2)}) copy-start(f32[384,768]{1,0:T(8,128)} %param.30) | copy-start | bytes 3538948
  85.0 83.0 %copy-start.60 = (s32[8,4,4]{0,2,1:T(4,128)S(1)}, s32[8,4,4]{0,2,1:T(4,128)}, u32[]{:S(2)}) copy-start(s32[8,4,4]{0,2,1:T(4,128)} %param.26) | copy-start | bytes 1540
  85.0 83.5 %copy-start.65 = (s32[8]{0:T(128)S(1)}, s32[8]{0:T(128)}, u32[]{:S(2)}) copy-start(s32[8]{0:T(128)} %param.25) | copy-start | bytes 100
  86.9 6.6 collective-permute-start
  93.4 38.4 %collective-permute-start.1 = (bf16[1024,1536]{1,0:T(8,128)(2,1)S(1)}, bf16[1024,1536]{1,0:T(8,128)(2,1)}, u32[]{:S(2)}, u32[]{:S(2)}) collective-permute-start(bf16[1024,1536]{1,0:T(8,128)(2,1)S(1)} %collective-permute-done), channel_id=1, source_target_pairs={{0,1},{1,2},{2,3},{4,5},{5,6},{6,7},{8,9},{9,10},{10,11},{12,13},{... | collective-permute-start | bytes 9437192 | tf_op jit(solution)/shard_map/ppermute | solution.py:28
  131.8 42.6 %collective-permute-start.2 = (bf16[1024,1536]{1,0:T(8,128)(2,1)}, bf16[1024,1536]{1,0:T(8,128)(2,1)}, u32[]{:S(2)}, u32[]{:S(2)}) collective-permute-start(bf16[1024,1536]{1,0:T(8,128)(2,1)} %collective-permute-done.1), channel_id=1, source_target_pairs={{0,1},{1,2},{2,3},{4,5},{5,6},{6,7},{8,9},{9,10},{10,11},{12,13},{... | collective-permute-start | bytes 9437192 | tf_op jit(solution)/shard_map/ppermute | solution.py:28
  167.6 552.6 %reduce-scatter.10.cloned.1.call-start = ((), (), s32[]{:S(2)}) async-start(), calls=%async_computation.10 | async-start | bytes 2654208 | tf_op jit(solution)/shard_map/reduce_scatter | solution.py:246
  317.8 402.4 %reduce-scatter.12.cloned.1.call-start = ((), (), s32[]{:S(2)}) async-start(), calls=%async_computation.11 | async-start | bytes 10616832 | tf_op jit(solution)/shard_map/reduce_scatter | solution.py:247
  337.1 383.1 %reduce-scatter.14.cloned.1.call-start = ((), (), s32[]{:S(2)}) async-start(), calls=%async_computation.12 | async-start | bytes 10616832 | tf_op jit(solution)/shard_map/reduce_scatter | solution.py:248
  516.9 30.3 %collective-permute-start.3 = (f32[1024,1536]{1,0:T(8,128)}, f32[1024,1536]{1,0:T(8,128)}, u32[]{:S(2)}, u32[]{:S(2)}) collective-permute-start(f32[1024,1536]{1,0:T(8,128)} %bitcast.232), channel_id=1, source_target_pairs={{1,0},{2,1},{3,2},{5,4},{6,5},{7,6},{9,8},{10,9},{11,10},{13,12},{... | collective-permute-start | bytes 18874376 | tf_op jit(solution)/shard_map/ppermute | solution.py:28
  531.2 361.4 %reduce-scatter.8.cloned.1.call-start = ((), (), s32[]{:S(2)}) async-start(), calls=%async_computation.9 | async-start | bytes 7962624 | tf_op jit(solution)/shard_map/reduce_scatter | solution.py:245
  555.9 54.5 %collective-permute-start.4 = (f32[1024,1536]{1,0:T(8,128)}, f32[1024,1536]{1,0:T(8,128)}, u32[]{:S(2)}, u32[]{:S(2)}) collective-permute-start(f32[1024,1536]{1,0:T(8,128)} %bitcast_add_fusion.2), channel_id=1, source_target_pairs={{1,0},{2,1},{3,2},{5,4},{6,5},{7,6},{9,8},{10,9},{11,10},{13,12},{... | collective-permute-start | bytes 18874376 | tf_op jit(solution)/shard_map/ppermute | solution.py:28
  573.2 47.3 %copy-start.32 = (bf16[2,4,128,12,64]{2,4,3,1,0:T(8,128)(2,1)S(1)}, bf16[2,4,128,12,64]{2,4,3,1,0:T(8,128)(2,1)}, u32[]{:S(2)}) copy-start(bf16[2,4,128,12,64]{2,4,3,1,0:T(8,128)(2,1)} %get-tuple-element.111) | copy-start | bytes 4718596
  619.2 73.4 %collective-permute-start.5 = (f32[1024,1536]{1,0:T(8,128)}, f32[1024,1536]{1,0:T(8,128)}, u32[]{:S(2)}, u32[]{:S(2)}) collective-permute-start(f32[1024,1536]{1,0:T(8,128)} %bitcast_add_fusion.1), channel_id=1, source_target_pairs={{1,0},{2,1},{3,2},{5,4},{6,5},{7,6},{9,8},{10,9},{11,10},{13,12},{... | collective-permute-start | bytes 18874376 | tf_op jit(solution)/shard_map/ppermute | solution.py:28
  623.9 74.3 %copy-start.19 = (bf16[1024,768]{1,0:T(8,128)(2,1)}, bf16[1024,768]{1,0:T(8,128)(2,1)S(1)}, u32[]{:S(2)}) copy-start(bf16[1024,768]{1,0:T(8,128)(2,1)S(1)} %copy.144) | copy-start | bytes 4718596
  640.0 59.9 %copy-start.28 = (bf16[1024,768]{1,0:T(8,128)(2,1)S(1)}, bf16[1024,768]{1,0:T(8,128)(2,1)}, u32[]{:S(2)}) copy-start(bf16[1024,768]{1,0:T(8,128)(2,1)} %copy-done.27) | copy-start | bytes 4718596
  705.8 251.4 %reduce-scatter.16.cloned.1.call-start = ((), (), s32[]{:S(2)}) async-start(), calls=%async_computation.13 | async-start | bytes 442368
  719.0 173.5 %copy-start.61 = (f32[768]{0:T(1024)S(1)}, f32[768]{0:T(1024)}, u32[]{:S(2)}) copy-start(f32[768]{0:T(1024)} %get-tuple-element.326) | copy-start | bytes 9220
  720.1 314.2 %all-reduce.3.cloned.1.call-start = ((), (), s32[]{:S(2)}) async-start(), calls=%async_computation.14 | async-start | bytes 7077888 | tf_op jit(solution)/shard_map/psum | solution.py:251
  906.2 57.9 %copy-start.53 = (f32[12,96]{1,0:T(8,128)S(1)}, f32[12,96]{1,0:T(8,128)}, u32[]{:S(2)}) copy-start(f32[12,96]{1,0:T(8,128)} %param.31) | copy-start | bytes 13828
  906.2 57.9 %copy-start.58 = (f32[12,96]{1,0:T(8,128)S(1)}, f32[12,96]{1,0:T(8,128)}, u32[]{:S(2)}) copy-start(f32[12,96]{1,0:T(8,128)} %param.36) | copy-start | bytes 13828
  906.2 57.9 %copy-start.59 = (f32[12,96]{1,0:T(8,128)S(1)}, f32[12,96]{1,0:T(8,128)}, u32[]{:S(2)}) copy-start(f32[12,96]{1,0:T(8,128)} %param.41) | copy-start | bytes 13828
  906.2 128.1 %copy-start.33 = (f32[96,768]{1,0:T(8,128)S(1)}, f32[96,768]{1,0:T(8,128)}, u32[]{:S(2)}) copy-start(f32[96,768]{1,0:T(8,128)} %param.28) | copy-start | bytes 884740
  906.2 128.1 %copy-start.40 = (f32[96,768]{1,0:T(8,128)S(1)}, f32[96,768]{1,0:T(8,128)}, u32[]{:S(2)}) copy-start(f32[96,768]{1,0:T(8,128)} %param.33) | copy-start | bytes 884740
  906.3 128.1 %copy-start.41 = (f32[96,768]{1,0:T(8,128)S(1)}, f32[96,768]{1,0:T(8,128)}, u32[]{:S(2)}) copy-start(f32[96,768]{1,0:T(8,128)} %param.38) | copy-start | bytes 884740
  906.3 130.1 %copy-start.25 = (f32[96,2304]{1,0:T(8,128)S(1)}, f32[96,2304]{1,0:T(8,128)}, u32[]{:S(2)}) copy-start(f32[96,2304]{1,0:T(8,128)} %param.27) | copy-start | bytes 2654212
  (54 other events, 426.9 us)
Sparse Core Ops, SparseCore 0:
  10.8 68.0 all-gather.5
  81.6 39.6 all-gather.7
  124.1 78.6 all-gather.9
  205.4 78.0 all-gather.11
  317.9 66.8 reduce-scatter.9
  388.3 162.4 reduce-scatter.11
  554.4 162.5 reduce-scatter.13
  720.7 171.8 reduce-scatter.7
  896.7 60.4 reduce-scatter.15
  959.9 74.4 all-reduce.2
where the time goes:
time: 1060 us; the launch traced here: 1050 us
  waiting for transfers between devices  450 us (42%)
  local copies, waits for them, and re-layouts  195 us (18%)
  matrix products  175 us (17%)
  other arithmetic  103 us (10%)
  starting transfers between devices  75.5 us (7%)
  blocking collectives  38.3 us (4%)
  between operations  15.4 us (1%)
    reduce_scatter x1, waiting for transfers between devices, body(): lax.psum_scatter(grad_qkv, 'items', scatter_dimension=0, tiled=True)  172 us
    ppermute x6, waiting for transfers between devices, from_behind(): return lax.ppermute(block, axis, route)  98.6 us
    slice x4, local copies, waits for them, and re-layouts, body(): carried = carried + slot_grads[hop]  90.5 us
    ppermute x6, starting transfers between devices, from_behind(): return lax.ppermute(block, axis, route)  74.8 us
    psum x1, waiting for transfers between devices, body(): lax.psum((shares[0], shares[1], shares[2], shares[3], shares[4]), 'blk')  69.6 us
    unnamed x11, waiting for transfers between devices  48.7 us
    all_gather x1, blocking collectives, body(): lax.all_gather(vectors.astype(bf), 'items', axis=1, tiled=True)  32.4 us
    all_gather x1, waiting for transfers between devices, body(): lax.all_gather(weight_qkv.astype(bf), 'items', axis=0, tiled=True)  30.8 us
  transfers between devices with their start and end apart: 16, of which 9 were waited for; matrix products, arithmetic and copies ran while one was open for 39% of the time, Pallas kernels for 0%

commit v1 on v0

v1 whole, which is shorter than its diff:
```python
import collections

import jax
import jax.numpy as jnp
from jax import lax
from jax.experimental import pallas as pl
from jax.experimental.pallas import tpu as pltpu
from jax.sharding import PartitionSpec as P

D = 768
H = 12
HD = 64
FF = 3072
GROUPS = 4
GROUP = 128
STEP = 5
CHUNKS = 3
WIDE = 1024
VROWS = 16
OWNERS = 8
MIB = 1024 * 1024

norm_eps = 1e-06
beta_one = 0.9
beta_two = 0.5
adam_eps = 1e-08
weight_decay = 0.1
rates = (0.1, 0.8, 0.1, 0.06, 1.0)
decays = (weight_decay, weight_decay, weight_decay, weight_decay, 0.0)
masked_value = -1e30

bf = jnp.bfloat16
f32 = jnp.float32
MESH = pl.DeviceIdType.MESH
ANY = pl.BlockSpec(memory_space=pl.ANY)
VMEM = pl.BlockSpec(memory_space=pltpu.VMEM)
SMEM = pl.BlockSpec(memory_space=pltpu.SMEM)
TOKENS = (GROUPS, 2, GROUP, D)


def adamw(weight, first, second, grad, rate, decay_rate):
    first_new = beta_one * first + (1.0 - beta_one) * grad
    second_new = beta_two * second + (1.0 - beta_two) * grad * grad
    first_hat = first_new * (1.0 / (1.0 - beta_one**STEP))
    second_hat = second_new * (1.0 / (1.0 - beta_two**STEP))
    weight_new = weight - rate * (
        first_hat / (jnp.sqrt(second_hat) + adam_eps) + decay_rate * weight
    )
    return (weight_new, first_new, second_new)


def nn(a, b):
    return jnp.dot(a, b, preferred_element_type=f32)


def nt(a, b):
    return lax.dot_general(a, b, (((1,), (1,)), ((), ())), preferred_element_type=f32)


def tn(a, b):
    return lax.dot_general(a, b, (((0,), (0,)), ((), ())), preferred_element_type=f32)


def normal(values):
    mean = jnp.mean(values, -1, keepdims=True)
    centred = values - mean
    scale = lax.rsqrt(jnp.mean(centred * centred, -1, keepdims=True) + norm_eps)
    return centred * scale, scale


def norm_back(grad, normed, scale, gain):
    e = grad * gain
    along = jnp.mean(e * normed, -1, keepdims=True)
    return scale * (e - jnp.mean(e, -1, keepdims=True) - normed * along)


def rows_of(ref, g):
    block = ref[g]
    return block.reshape(2 * GROUP, block.shape[-1])


def halves(ref, k):
    block = ref[2 * k : 2 * k + 2]
    return block.reshape(512, block.shape[-1])


def put_rows(ref, g, values):
    ref[g] = values.reshape(2, GROUP, values.shape[-1])


def span256(g):
    return pl.ds(pl.multiple_of(g * 256, 256), 256)


def col_sum(values):
    return jnp.sum(values, 0, keepdims=True)


def stacked(pair, low):
    zero = jnp.zeros_like(pair)
    return jnp.concatenate([jnp.where(low, pair, zero), jnp.where(low, zero, pair)], 0)


def run_hooks(hooks, index):
    for at, hook in hooks.items():
        pl.when(index == at)(hook)


def up_block(c, i):
    lane = 3 * (i % 2) + c
    return slice(8 + i // 2, 9 + i // 2), slice(lane * 128, (lane + 1) * 128)


LAYER_BUFFERS = dict(
    x=(TOKENS, bf),
    dy=(TOKENS, bf),
    qkv=(TOKENS[:3] + (3 * D,), bf),
    o=(TOKENS, bf),
    x2=(TOKENS, f32),
    a2=(TOKENS, bf),
    a2t=((D, 1024), bf),
    dyt=((D, 1024), bf),
    gl=((1024, WIDE), bf),
    du=((1024, WIDE), bf),
    yacc=(TOKENS, f32),
    da2=(TOKENS, f32),
    dkv=((2, GROUPS * GROUP, 128), f32),
    eye=((256, 256), bf),
    stats=((H, GROUPS, 256), f32),
    vec=((VROWS, D), f32),
    bu=((CHUNKS, 1, WIDE), f32),
    gbu=((CHUNKS, 1, WIDE), f32),
    bqkv=((3, 1, D), f32),
    gv=((VROWS, D), f32),
    wqkv=((3, 4, 2, 2, 48, D), bf),
    wo=((4, 2, 2, 48, D), bf),
    wup=((CHUNKS, 4, 2, 2, 48, WIDE), bf),
    wdn=((CHUNKS, 4, 2, 2, 64, D), bf),
    gdn=((CHUNKS, 4, 2, 2, 384, 128), bf),
)


class Masks:
    def __init__(self, counts, masks):
        self.counts, self.masks, self.first = counts, masks, lax.axis_index("blk") * 2
        self.place = lax.broadcasted_iota(jnp.int32, (GROUP, 256), 0)

    def __call__(self, s, t, g):
        item = self.first + t
        open_first = self.masks[g, 0, item] * self.counts[item]
        parts = [jnp.where(self.place < open_first, s[:GROUP], masked_value)]
        for k in range(1, g + 1):
            part = s[k * GROUP : (k + 1) * GROUP]
            if k < g:
                part = part + (self.masks[g, k, item] - 1).astype(f32) * -masked_value
            parts.append(part)
        return jnp.concatenate(parts, 0)


class Layer:
    def __init__(self, refs, masks):
        self.r, self.masks = refs, masks
        self.low = lax.broadcasted_iota(jnp.int32, (1, 2 * HD), 1) < HD
        self.upper = lax.broadcasted_iota(jnp.int32, (2 * HD, 1), 0) < HD

    def start(self):
        r = self.r
        row = lax.broadcasted_iota(jnp.int32, (256, 256), 0)
        col = lax.broadcasted_iota(jnp.int32, (256, 256), 1)
        r.eye[...] = jnp.where(row == col, 1.0, 0.0).astype(bf)
        r.gv[...] = jnp.zeros_like(r.gv)
        r.gbu[...] = jnp.zeros_like(r.gbu)

    def turned(self, values):
        n = values.shape[1]
        return nt(self.r.eye[:n, :n], values).astype(bf)

    def turn_rows(self, ref, g, values):
        for m in range(3):
            ref[m * 256 : (m + 1) * 256, span256(g)] = self.turned(values[:, m * 256 : (m + 1) * 256])

    def own_heads(self, pair):
        return self.turned(jnp.where(self.upper, pair[:, :GROUP], pair[:, GROUP:]).astype(bf)).astype(bf)

    def qkv_grad(self, hq):
        return self.r.wdn.at[hq, :, :, :, pl.ds(0, 48), :]

    def vec(self, k):
        return self.r.vec[k : k + 1, :]

    def spread_biases(self):
        r = self.r
        for hq in range(3):
            for w, k in ((0, 4), (2, 5)):
                r.bqkv[hq, :, w * 256 : w * 256 + 256] = r.vec[k : k + 1, hq * 256 : hq * 256 + 256]
            r.bqkv[hq, :, 256:512] = jnp.zeros((1, 256), f32)
        for c in range(CHUNKS):
            for i in range(OWNERS):
                r.bu[c, :, i * 128 : (i + 1) * 128] = r.vec[up_block(c, i)]

    def first_norm(self, g):
        normed, _ = normal(rows_of(self.r.x, g).astype(f32))
        return (normed * self.vec(0) + self.vec(1)).astype(bf)

    def norm_item(self, t):
        r = self.r

        def step(g, _):
            normed, _ = normal(r.x[g, t].astype(f32))
            r.a2[g, t] = (normed * self.vec(0) + self.vec(1)).astype(bf)
            return 0

        lax.fori_loop(0, GROUPS, step, 0)

    def lanes(self, hq, hp, w):
        return pl.ds(pl.multiple_of(hq * D + w * 256 + hp * 128, 128), 128)

    def attend(self, part, hooks):
        r, low = self.r, self.low
        t, hq = part // 3, part % 3
        a1 = r.a2[:, t].reshape(GROUPS * GROUP, D)
        p = nn(a1, r.wqkv[hq].reshape(D, D)) + self.qkv_bias(hq)
        r.qkv[:, t, :, pl.ds(pl.multiple_of(hq * D, 128), D)] = p.astype(bf).reshape(GROUPS, GROUP, D)
        run_hooks(hooks, 3 * part)

        def step(hp, _):
            lanes = [self.lanes(hq, hp, w) for w in range(3)]
            out = pl.ds(pl.multiple_of(hq * 256 + hp * 128, 128), 128)
            k2 = r.qkv[:, t, :, lanes[1]].reshape(GROUPS * GROUP, 128)
            v2 = self.turned(r.qkv[:, t, :, lanes[2]].reshape(GROUPS * GROUP, 128))
            for g in range(GROUPS):
                n = (g + 1) * GROUP
                qs = stacked(r.qkv[g, t, :, lanes[0]] * jnp.asarray(0.125, bf), low)
                s = self.masks(nt(k2[:n], qs), t, g)
                top = jnp.max(s, 0, keepdims=True)
                e = jnp.exp(s - top)
                total = jnp.sum(e, 0, keepdims=True)
                p = (e * (1.0 / total)).astype(bf)
                r.stats[6 * t + 2 * hq + hp, g : g + 1, :] = top + jnp.log(total)
                r.o[g, t, :, out] = self.own_heads(nn(v2[:, :n], p))
            run_hooks(hooks, 3 * part + 1 + hp)
            return 0

        lax.fori_loop(0, 2, step, 0)

    def qkv_bias(self, hq):
        return self.r.bqkv[hq]

    def middle(self, hooks):
        r = self.r

        def step(g, _):
            v = rows_of(r.x, g).astype(f32) + nn(rows_of(r.o, g), r.wo[...].reshape(D, D)) + self.vec(6)
            put_rows(r.x2, g, v)
            put_rows(r.yacc, g, v + self.vec(7))
            normed, _ = normal(v)
            a = (normed * self.vec(2) + self.vec(3)).astype(bf)
            put_rows(r.a2, g, a)
            self.turn_rows(r.a2t, g, a)
            dy = rows_of(r.dy, g)
            self.turn_rows(r.dyt, g, dy)
            put_rows(r.da2, g, jnp.zeros((256, D), f32))
            r.gv[7:8, :] += col_sum(dy.astype(f32))
            run_hooks(hooks, g)
            return 0

        lax.fori_loop(0, GROUPS, step, 0)

    def feed(self, hooks):
        r = self.r

        def column(c, j):
            cols = span256(j)
            wup = r.wup[c, :, :, :, :, cols].reshape(D, 256)
            wdn = r.wdn[c, j].reshape(256, D)
            for k in range(2):
                rows = slice(512 * k, 512 * k + 512)
                u = nn(halves(r.a2, k), wup) + r.bu[c, :, cols]
                u2 = u * u
                half = 0.5 * jnp.tanh(u * (0.7978845608028654 + 0.035677408136300125 * u2)) + 0.5
                r.gl[rows, cols] = (u * half).astype(bf)
                slope = half + u * (2.0 * half * (1.0 - half)) * (
                    0.7978845608028654 + 0.10703222440890037 * u2
                )
                d = (nt(halves(r.dy, k), wdn) * slope).astype(bf)
                r.du[rows, cols] = d
                r.gbu[c, :, cols] += col_sum(d.astype(f32))

        def chunk(c, _):
            def step(j, _):
                column(c, j)
                run_hooks(hooks, 10 * c + j)
                return 0

            def down_grad(h, _):
                down = nn(r.dyt[pl.ds(pl.multiple_of(h * 384, 384), 384), :], r.gl[...]).astype(bf)
                for i in range(OWNERS):
                    r.gdn[c, i // 2, i % 2, h] = down[:, i * 128 : (i + 1) * 128]
                return 0

            def up_back(k, _):
                rows = pl.ds(pl.multiple_of(512 * k, 512), 512)
                back = nt(r.du[rows, :], r.wup[c].reshape(D, WIDE))
                r.da2[pl.ds(2 * k, 2)] += back.reshape(2, 2, GROUP, D)
                return 0

            def up_grad(h, _):
                up = nn(r.a2t[pl.ds(pl.multiple_of(h * 384, 384), 384), :], r.du[...]).astype(bf)
                r.wup[c, pl.ds(2 * h, 2)] = up.reshape(2, 2, 2, 48, WIDE)
                return 0

            def down(k, _):
                rows = pl.ds(pl.multiple_of(512 * k, 512), 512)
                out = nn(r.gl[rows, :], r.wdn[c].reshape(WIDE, D))
                r.yacc[pl.ds(2 * k, 2)] += out.reshape(2, 2, GROUP, D)
                return 0

            lax.fori_loop(0, 4, step, 0)
            for n, act in enumerate((down_grad, up_back, up_grad, down)):
                lax.fori_loop(0, 2, act, 0)
                run_hooks(hooks, 10 * c + 4 + n)
            return 0

        lax.fori_loop(0, CHUNKS, chunk, 0)
        for c in range(CHUNKS):
            for i in range(OWNERS):
                r.gv[up_block(c, i)] = r.gbu[c, :, i * 128 : (i + 1) * 128]

    def turn(self, order, send, hooks):
        r = self.r

        def step(k, _):
            g = order(k)
            c = rows_of(r.da2, g)
            normed, scale = normal(rows_of(r.x2, g))
            r.gv[2:3, :] += col_sum(c * normed)
            r.gv[3:4, :] += col_sum(c)
            d = rows_of(r.dy, g).astype(f32) + norm_back(c, normed, scale, self.vec(2))
            put_rows(r.dy, g, rows_of(r.yacc, g).astype(bf))
            send(k, g)
            put_rows(r.da2, g, d)
            r.gv[6:7, :] += col_sum(d)
            dz = d.astype(bf)
            put_rows(r.a2, g, dz)
            self.turn_rows(r.gl, g, rows_of(r.o, g))
            self.turn_rows(r.du, g, self.first_norm(g))
            put_rows(r.yacc, g, jnp.zeros((256, D), f32))
            run_hooks(hooks, k)
            return 0

        lax.fori_loop(0, GROUPS, step, 0)

    def out_grads(self):
        r = self.r

        def back(k, _):
            rows = pl.ds(2 * k, 2)
            do = nt(r.a2[rows].reshape(512, D), r.wo[...].reshape(D, D)).astype(bf)
            r.o[rows] = do.reshape(2, 2, GROUP, D)
            return 0

        def grad(h, _):
            part = r.gl[pl.ds(pl.multiple_of(h * 384, 384), 384), :]
            grads = nn(part, r.a2[...].reshape(GROUPS * 256, D)).astype(bf)
            r.wo[pl.ds(2 * h, 2)] = grads.reshape(2, 2, 2, 48, D)
            return 0

        lax.fori_loop(0, 2, back, 0)
        lax.fori_loop(0, 2, grad, 0)

    def attend_back(self, hooks, order, send):
        r, low = self.r, self.low

        def pair(hq, t, hp):
            lanes = [self.lanes(hq, hp, w) for w in range(3)]
            out = pl.ds(pl.multiple_of(hq * 256 + hp * 128, 128), 128)
            r.dkv[...] = jnp.zeros_like(r.dkv)
            k2 = r.qkv[:, t, :, lanes[1]].reshape(GROUPS * GROUP, 128)
            v2 = r.qkv[:, t, :, lanes[2]].reshape(GROUPS * GROUP, 128)
            turned_k = self.turned(k2)
            for g in range(GROUPS):
                n = (g + 1) * GROUP
                qs = stacked(r.qkv[g, t, :, lanes[0]] * jnp.asarray(0.125, bf), low)
                dos = stacked(r.o[g, t, :, out], low)
                s = self.masks(nt(k2[:n], qs), t, g)
                p = jnp.exp(s - r.stats[6 * t + 2 * hq + hp, g : g + 1, :])
                dp = nt(v2[:n], dos)
                ds = (p * (dp - jnp.sum(p * dp, 0, keepdims=True))).astype(bf)
                r.dkv[0, :n, :] += nn(ds, qs)
                r.dkv[1, :n, :] += nn(p.astype(bf), dos)
                r.qkv[g, t, :, lanes[0]] = self.own_heads(nn(turned_k[:, :n], ds) * 0.125)
            for w in range(2):
                r.qkv[:, t, :, lanes[w + 1]] = r.dkv[w].astype(bf).reshape(GROUPS, GROUP, 128)

        def quad(hq, _):
            cols = pl.ds(pl.multiple_of(hq * D, 128), D)

            def item(t, _):
                def step(hp, _):
                    pair(hq, t, hp)
                    run_hooks(hooks, 10 * hq + 2 * t + hp)
                    return 0

                lax.fori_loop(0, 2, step, 0)
                pl.when(t == 1)(lambda: grads(hq, cols))
                run_hooks(hooks, 10 * hq + 4 + t)
                rows = r.qkv[:, t, :, cols].reshape(512, D)
                back = nt(rows, r.wqkv[hq].reshape(D, D))
                r.yacc[:, t] += back.reshape(GROUPS, GROUP, D)
                run_hooks(hooks, 10 * hq + 6 + t)

                @pl.when(hq == 2)
                def _():
                    lax.fori_loop(0, GROUPS, lambda k, _: finish(t, k), 0)
                    run_hooks(hooks, 10 * hq + 8 + t)

                return 0

            lax.fori_loop(0, 2, item, 0)
            return 0

        def grads(hq, cols):
            d = r.qkv[:, :, :, cols].reshape(GROUPS * 256, D)

            def grad(h, _):
                part = r.du[pl.ds(pl.multiple_of(h * 384, 384), 384), :]
                out = nn(part, d).astype(bf)
                r.wdn[hq, pl.ds(2 * h, 2), :, :, :48, :] = out.reshape(2, 2, 2, 48, D)
                return 0

            lax.fori_loop(0, 2, grad, 0)
            sums = col_sum(d.astype(f32))
            r.gv[4:5, span256(hq)] = sums[:, :256]
            r.gv[5:6, span256(hq)] = sums[:, 512:]

        def finish(t, k):
            g = order(k)
            c = r.yacc[g, t]
            normed, scale = normal(r.x[g, t].astype(f32))
            r.gv[0:1, :] += col_sum(c * normed)
            r.gv[1:2, :] += col_sum(c)
            d = r.da2[g, t] + norm_back(c, normed, scale, self.vec(0))
            r.x[g, t] = d.astype(bf)
            send(k, t)
            return 0

        lax.fori_loop(0, 3, quad, 0)


class Here:
    def __init__(self):
        self.i, self.b = lax.axis_index("items"), lax.axis_index("blk")
        self.z, self.y = self.i // 2, self.i % 2
        self.x, self.c = self.b // 2, self.b % 2

    def z_plus(self, k):
        return (self.z + k) % 4

    def at_z(self, k):
        return (2 * self.z_plus(k) + self.y, self.b)

    def at_y(self):
        return (self.i + 1 - 2 * self.y, self.b)

    def at_x(self):
        return (self.i, (self.b + 2) % 4)

    def at_core(self):
        return (self.i, self.b + 1 - 2 * self.c)

    def at_blk(self, k):
        return (self.i, (self.b + k) % 4)

    def at_items(self, k):
        return ((self.i + k) % OWNERS, self.b)


def remote(src, dst, send, recv, device):
    return pltpu.make_async_remote_copy(
        src_ref=src, dst_ref=dst, send_sem=send, recv_sem=recv, device_id=device, device_id_type=MESH
    )


class Mail:
    def __init__(self, here, send, recv):
        self.here, self.send, self.recv = here, send, recv

    def go(self, src, dst, slot, device):
        remote(src, dst, self.send.at[slot], self.recv.at[slot], device).start()

    def arrived(self, dst, slot):
        remote(dst, dst, self.send.at[slot], self.recv.at[slot], self.here.at_core()).wait_recv()

    def left(self, src, *slots):
        for slot in slots:
            remote(src, src, self.send.at[slot], self.recv.at[slot], self.here.at_core()).wait_send()


class Gather(Mail):
    slots = 5

    def __init__(self, here, dst, send, recv):
        super().__init__(here, send, recv)
        self.dst = dst

    def first(self):
        h = self.here
        own = self.dst.at[h.z, h.y, h.c]
        for k in (1, 2, 3):
            self.go(own, own, k - 1, h.at_z(k))

    def second(self):
        h = self.here
        for k in (1, 2, 3):
            self.arrived(self.dst.at[h.z_plus(4 - k), h.y, h.c], k - 1)
        line = self.dst.at[:, h.y, h.c]
        self.go(line, line, 3, h.at_y())

    def third(self):
        h = self.here
        self.arrived(self.dst.at[:, 1 - h.y, h.c], 3)
        half = self.dst.at[:, :, h.c]
        self.go(half, half, 4, h.at_core())

    def last(self):
        self.arrived(self.dst.at[:, :, 1 - self.here.c], 4)

    def drain(self):
        self.left(self.dst.at[0, 0, 0], 0, 1, 2)
        self.left(self.dst.at[:, 0, 0], 3)
        self.left(self.dst.at[:, :, 0], 4)


class SplitGather(Gather):
    slots = 6

    def mine(self, z, y):
        h = self.here
        return self.dst.at[z, y, h.c, :, self.columns(h.x)]

    def columns(self, x):
        width = self.dst.shape[-1] // 2
        return pl.ds(pl.multiple_of(x * width, width), width)

    def first(self):
        h = self.here
        own = self.mine(h.z, h.y)
        for k in (1, 2, 3):
            self.go(own, own, k - 1, h.at_z(k))

    def second(self):
        h = self.here
        for k in (1, 2, 3):
            self.arrived(self.mine(h.z_plus(4 - k), h.y), k - 1)
        line = self.mine(slice(None), h.y)
        self.go(line, line, 3, h.at_y())

    def across(self):
        h = self.here
        self.arrived(self.mine(slice(None), 1 - h.y), 3)
        part = self.mine(slice(None), slice(None))
        self.go(part, part, 5, h.at_x())

    def third(self):
        h = self.here
        self.arrived(self.dst.at[:, :, h.c, :, self.columns(1 - h.x)], 5)
        half = self.dst.at[:, :, h.c]
        self.go(half, half, 4, h.at_core())

    def drain(self):
        self.left(self.mine(0, 0), 0, 1, 2)
        self.left(self.mine(slice(None), 0), 3)
        self.left(self.dst.at[:, :, 0], 4)
        self.left(self.mine(slice(None), slice(None)), 5)


class Exchange(Mail):
    def __init__(self, here, src, dst, send, recv, local):
        super().__init__(here, send, recv)
        self.src, self.dst, self.local = src, dst, local

    def own(self):
        h = self.here
        return pltpu.make_async_copy(self.src.at[h.b], self.dst.at[h.b], self.local)

    def order(self, k):
        h = self.here
        odd, near = k % 2, k // 2
        far = (1 - odd) * ((h.b + 2) % 4) + odd * (3 - h.b)
        return (1 - near) * far + near * (h.b + (1 - odd) * (1 - 2 * h.c))

    def copy(self, k):
        h = self.here
        to = self.order(k)
        return remote(self.src.at[to], self.dst.at[h.b], self.send.at[k], self.recv.at[k], (h.i, to))

    def put(self, k, _=None):
        @pl.when(k < 3)
        def _():
            self.copy(k).start()

        @pl.when(k == 3)
        def _():
            self.own().start()

    def start(self):
        for k in range(3):
            self.copy(k).start()
        self.own().start()

    def arrive(self):
        self.own().wait()
        for k in range(3):
            self.arrived(self.dst.at[self.order(k)], k)

    def drain(self):
        for k in range(3):
            self.copy(k).wait_send()


class ItemExchange(Exchange):
    def copy(self, k, t):
        h = self.here
        to, slot = self.order(k), 3 * t + k
        return remote(
            self.src.at[to, t], self.dst.at[h.b, t], self.send.at[slot], self.recv.at[slot], (h.i, to)
        )

    def own(self, t):
        h = self.here
        return pltpu.make_async_copy(self.src.at[h.b, t], self.dst.at[h.b, t], self.local.at[t])

    def put(self, k, t):
        @pl.when(k < 3)
        def _():
            self.copy(k, t).start()

        @pl.when(k == 3)
        def _():
            self.own(t).start()

    def start(self):
        for t in range(2):
            for k in range(3):
                self.copy(k, t).start()
            self.own(t).start()

    def arrive(self, t):
        self.own(t).wait()
        for k in range(3):
            self.arrived(self.dst.at[self.order(k), t], 3 * t + k)

    def drain(self):
        self.left(self.src.at[0, 0], *range(6))


class Reduce(Mail):
    slots = 8

    def __init__(self, here, g, rc, place, count, credit, ry, rz, rx, total, out, send, recv):
        super().__init__(here, send, recv)
        self.g, self.rc, self.place, self.count, self.credit = g, rc, place, count, credit
        self.ry, self.rz, self.rx, self.total, self.out = ry, rz, rx, total, out

    def over_core(self):
        h = self.here
        if self.place is not None and self.place >= 2:
            pl.semaphore_wait(self.credit, 1)
        self.go(self.g.at[:, :, 1 - h.c], self.rc, 0, h.at_core())

    def over_y(self):
        h = self.here
        self.arrived(self.rc, 0)

        def add(n, _):
            z, y = n // 2, n % 2
            self.g[z, y, h.c] = self.g[z, y, h.c] + self.rc[z, y]
            return 0

        lax.fori_loop(0, 8, add, 0)
        if self.place is not None and self.place + 2 < self.count:
            pl.semaphore_signal(self.credit, inc=1, device_id=h.at_core(), device_id_type=MESH)
        self.go(self.g.at[:, 1 - h.y, h.c], self.ry, 1, h.at_y())

    def over_z(self):
        h = self.here
        self.arrived(self.ry, 1)

        def add(z, _):
            self.g[z, h.y, h.c] = self.g[z, h.y, h.c] + self.ry[z]
            return 0

        lax.fori_loop(0, 4, add, 0)
        for k in (2, 1, 3):
            self.go(self.g.at[h.z_plus(k), h.y, h.c], self.rz.at[k - 1], 1 + k, h.at_z(k))

    def over_x(self):
        h = self.here
        part = self.g[h.z, h.y, h.c].astype(f32)
        for k in (1, 2, 3):
            self.arrived(self.rz.at[k - 1], 1 + k)
            part = part + self.rz[k - 1].astype(f32)
        self.total[0] = part.astype(bf)
        self.go(self.total.at[0], self.rx, 5, h.at_x())

    def share(self):
        h = self.here
        self.arrived(self.rx, 5)
        self.total[1] = self.total[0] + self.rx[...]
        self.own().start()
        self.go(self.total.at[1], self.out.at[h.c], 6, h.at_core())

    def own(self):
        return pltpu.make_async_copy(self.total.at[1], self.out.at[self.here.c], self.send.at[7])

    def last(self):
        self.arrived(self.out.at[1 - self.here.c], 6)
        self.own().wait()

    def drain(self):
        self.left(self.rc, 0)
        self.left(self.ry, 1)
        self.left(self.rz.at[0], 2, 3, 4)
        self.left(self.rx, 5, 6)


class SplitReduce(Reduce):
    slots = 9

    def __init__(self, rx0, *args):
        super().__init__(*args)
        self.rx0 = rx0

    def rows(self, x):
        count = self.g.shape[-2] // 2
        return pl.ds(pl.multiple_of(x * count, count), count)

    def over_x0(self):
        h = self.here
        self.arrived(self.rc, 0)

        def add(n, _):
            z, y = n // 2, n % 2
            self.g[z, y, h.c] = self.g[z, y, h.c] + self.rc[z, y]
            return 0

        lax.fori_loop(0, 8, add, 0)
        if self.place + 2 < self.count:
            pl.semaphore_signal(self.credit, inc=1, device_id=h.at_core(), device_id_type=MESH)
        self.go(self.g.at[:, :, h.c, self.rows(1 - h.x)], self.rx0, 8, h.at_x())

    def over_y(self):
        h = self.here
        mine = self.rows(h.x)
        self.arrived(self.rx0, 8)

        def add(n, _):
            z, y = n // 2, n % 2
            self.g[z, y, h.c, mine] = self.g[z, y, h.c, mine] + self.rx0[z, y]
            return 0

        lax.fori_loop(0, 8, add, 0)
        self.go(self.g.at[:, 1 - h.y, h.c, mine], self.ry.at[:, self.rows(0)], 1, h.at_y())

    def over_z(self):
        h = self.here
        mine, box = self.rows(h.x), self.rows(0)
        self.arrived(self.ry.at[:, box], 1)

        def add(z, _):
            self.g[z, h.y, h.c, mine] = self.g[z, h.y, h.c, mine] + self.ry[z, box]
            return 0

        lax.fori_loop(0, 4, add, 0)
        for k in (2, 1, 3):
            self.go(self.g.at[h.z_plus(k), h.y, h.c, mine], self.rz.at[k - 1, box], 1 + k, h.at_z(k))

    def over_x(self):
        h = self.here
        mine, box = self.rows(h.x), self.rows(0)
        part = self.g[h.z, h.y, h.c, mine].astype(f32)
        for k in (1, 2, 3):
            self.arrived(self.rz.at[k - 1, box], 1 + k)
            part = part + self.rz[k - 1, box].astype(f32)
        self.total[1, mine] = part.astype(bf)
        done = self.total.at[1, mine]
        self.go(done, done, 5, h.at_x())

    def share(self):
        h = self.here
        self.arrived(self.total.at[1, self.rows(1 - h.x)], 5)
        self.own().start()
        self.go(self.total.at[1], self.out.at[h.c], 6, h.at_core())

    def drain(self):
        box = self.rows(0)
        self.left(self.rc, 0)
        self.left(self.ry.at[:, box], 1)
        self.left(self.rz.at[0, box], 2, 3, 4)
        self.left(self.total.at[1, box], 5)
        self.left(self.rx, 6)
        self.left(self.rx0, 8)


WINDOW = 256


def window_start(owner):
    return (3 * owner // 4 - owner // 7) * 128


def window_of(owner):
    return pl.ds(pl.multiple_of(window_start(owner), 128), WINDOW)


class ReduceVectors(Mail):
    def __init__(self, here, v, blk_inbox, items_inbox, out, send, recv):
        super().__init__(here, send, recv)
        self.v, self.blk_inbox, self.items_inbox, self.out = v, blk_inbox, items_inbox, out

    def first(self):
        h = self.here
        self.blk_inbox[h.b] = self.v[...]
        for k in (1, 2, 3):
            self.go(self.v, self.blk_inbox.at[h.b], k - 1, h.at_blk(k))

    def second(self):
        h = self.here
        for k in (1, 2, 3):
            self.arrived(self.blk_inbox.at[(h.b + 4 - k) % 4], k - 1)
        self.left(self.v, 0, 1, 2)
        box = self.blk_inbox
        self.v[...] = (box[0] + box[1]) + (box[2] + box[3])
        for k in range(1, OWNERS):
            owner = (h.i + k) % OWNERS
            self.go(
                self.v.at[:, window_of(owner)], self.items_inbox.at[h.i], 2 + k, h.at_items(k)
            )
        self.items_inbox[h.i] = self.v[:, window_of(h.i)]

    def third(self):
        h = self.here
        for k in range(1, OWNERS):
            self.arrived(self.items_inbox.at[(h.i + OWNERS - k) % OWNERS], 2 + k)
        total = self.items_inbox[0]
        for n in range(1, OWNERS):
            total = total + self.items_inbox[n]
        self.out[...] = total

    def drain(self):
        self.left(self.out, *range(3, 10))


INBOXES = (("d", CHUNKS, 384, 128), ("u", CHUNKS, 48, WIDE), ("q", 4, 48, D))
COMM_BUFFERS = dict(
    rcd=((2, 4, 2, 384, 128), bf),
    rcu=((2, 4, 2, 48, WIDE), bf),
    vbox=((OWNERS, VROWS, WINDOW), bf),
    gbox=((GROUPS, VROWS, D), f32),
    wbox=((OWNERS, VROWS, WINDOW), f32),
    gvw=((VROWS, WINDOW), f32),
    rx0=((2, 4, 2, 192, 128), bf),
)
for _kind, _n, _rows, _cols in INBOXES:
    COMM_BUFFERS["ry" + _kind] = ((_n, 4, _rows, _cols), bf)
    COMM_BUFFERS["rz" + _kind] = ((_n, 3, _rows, _cols), bf)
    COMM_BUFFERS["rx" + _kind] = ((_n, _rows, _cols), bf)
    COMM_BUFFERS["tt" + _kind] = ((_n, 2, _rows, _cols), bf)
SEMS = dict(
    load=(11,),
    gsend=(13, SplitGather.slots),
    grecv=(13, SplitGather.slots),
    rsend=(12, SplitReduce.slots),
    rrecv=(12, SplitReduce.slots),
    xsend=(2, 6),
    xrecv=(2, 6),
    xlocal=(2, 2),
    esend=(2, 3),
    erecv=(2, 3),
    local=(5,),
    vsend=(7,),
    vrecv=(7,),
    wsend=(10,),
    wrecv=(10,),
)


SPLIT_UP = (0, 1, 2)
SPLIT_DOWN = (1, 2)
MOVES = dict(
    a="first", l="second", xx="across", h="third", w="last",
    core="over_core", x0="over_x0", y="over_y", z="over_z", x="over_x", sh="share", end="last",
)
TIMETABLE = dict(
    start=(("Q0q", "a"), ("Q0k", "a"), ("Q0v", "a"),),
    table=(("Q0q", "l"), ("Q0k", "l"), ("Q1", "a"), ("Q0q", "h"), ("Q0v", "l"), ("Q2", "a"), ("Q0k", "h"), ("Q0q", "w"),),
    ln0=(("Q0v", "h"), ("Q0k", "w"), ("Q0v", "w"),),
    s0a=(("Q1", "l"), ("O", "a"),),
    s0b=(("Q2", "l"), ("U0", "a"), ("Q1", "h"), ("Q1", "w"),),
    s1p=(("O", "l"), ("D0", "a"),),
    s1b=(("Q2", "h"), ("U0", "l"), ("U1", "a"), ("Q2", "w"),),
    s2a=(("O", "h"),),
    s3a=(("O", "w"), ("U0", "xx"), ("D0", "l"), ("D1", "a"),),
    s4b=(("U1", "l"), ("U2", "a"),),
    m1=(("U0", "h"), ("D0", "h"),),
    m3=(("D1", "l"), ("D2", "a"), ("U0", "w"), ("U1", "xx"), ("D0", "w"),),
    f00=(("U2", "l"),),
    f03=(("D1", "h"),),
    g00=(("U1", "h"), ("d0", "core"),),
    g01=(("D1", "w"), ("U2", "xx"), ("D2", "l"),),
    g02=(("U1", "w"), ("u0", "core"),),
    f10=(("d0", "y"),),
    f11=(("u0", "y"),),
    f13=(("U2", "h"), ("D2", "h"),),
    g10=(("d1", "core"),),
    g11=(("U2", "w"),),
    g12=(("u1", "core"),),
    g13=(("D2", "w"), ("d0", "z"),),
    f20=(("d1", "x0"),),
    f21=(("u1", "y"),),
    g20=(("u0", "z"), ("d2", "core"),),
    g21=(("d0", "x"),),
    g22=(("d1", "y"), ("d2", "x0"), ("u2", "core"),),
    g23=(("d0", "sh"),),
    t1=(("u1", "z"), ("u2", "y"), ("d0", "end"),),
    t3=(("u0", "x"),),
    gwo=(("d1", "z"), ("o", "core"),),
    b00=(("d2", "y"),),
    b01=(("o", "y"),),
    b02=(("u1", "x"),),
    b03=(("u2", "z"),),
    gq0=(("d1", "x"), ("q0", "core"),),
    b10=(("d2", "z"),),
    b11=(("q0", "y"),),
    b13=(("o", "z"), ("u2", "x"),),
    gq1=(("q1", "core"),),
    on11=(("u0", "sh"),),
    b20=(("u1", "sh"), ("d2", "x"),),
    b21=(("u0", "end"), ("d1", "sh"), ("u1", "end"), ("q0", "z"), ("q1", "y"),),
    on20=(("u2", "sh"), ("d1", "end"),),
    fin0=(("d2", "sh"),),
    b22=(("u2", "end"), ("o", "x"), ("d2", "end"),),
    gq2=(("q2q", "core"), ("q2k", "core"), ("q2v", "core"),),
    on21=(("q1", "z"),),
    fin1=(("q2q", "y"), ("q2k", "y"), ("q0", "x"),),
    tail0=(("q2v", "y"), ("o", "sh"), ("q2q", "z"), ("o", "end"), ("q2k", "z"), ("q1", "x"), ("q2v", "z"), ("q2q", "x"), ("q2k", "x"), ("q0", "sh"), ("q2v", "x"),),
    tail1=(("q0", "end"), ("q1", "sh"), ("q2q", "sh"), ("q2k", "sh"), ("q2v", "sh"), ("q1", "end"), ("q2q", "end"),),
    tail2=(("q2k", "end"), ("q2v", "end"),),
)


def step_kernel(*refs):
    (xs, dys, counts, masks, w_qkv, w_o, w_up, w_dn, w_vec, y, dx, gv, o_dn, o_up, o_o, o_q) = refs[:16]
    names = list(LAYER_BUFFERS) + list(COMM_BUFFERS) + list(SEMS) + ["credit_d", "credit_u"]
    r = collections.namedtuple("Refs", names)(*refs[16:])
    here = Here()
    barrier = pltpu.get_barrier_semaphore()
    friends = [here.at_items(k) for k in range(1, OWNERS)] + [here.at_blk(k) for k in (1, 2, 3)]
    for device in friends:
        pl.semaphore_signal(barrier, inc=1, device_id=device, device_id_type=MESH)

    half = pl.ds(here.c * 48, 48)
    small, small_dn = pl.ds(0, 48), pl.ds(0, 64)
    loads = []
    for q in range(3):
        loads.append((w_qkv.at[half, pl.ds(q * D, D)], r.x2.at[q // 2, q % 2, small, :]))
    loads.append((w_o.at[half], r.x2.at[1, 1, small, :]))
    for q in range(4):
        loads.append((w_up.at[half, pl.ds(q * D, D)], r.x2.at[2 + q // 2, q % 2, small, :]))
    for q in range(3):
        rows = pl.ds(q * 128 + here.c * 64, 64)
        loads.append((w_dn.at[rows], r.yacc.at[q // 2, q % 2, small_dn, :]))
    loads = [pltpu.make_async_copy(s, d, r.load.at[n]) for n, (s, d) in enumerate(loads)]
    for load in loads:
        load.start()

    layer = Layer(r, Masks(counts, masks))
    for q in range(3):
        loads[q].wait()
        part = r.x2[q // 2, q % 2, :48, :].astype(bf)
        for hq in range(3):
            r.wqkv[hq, here.z, here.y, here.c, :, q * 256 : q * 256 + 256] = part[:, hq * 256 : hq * 256 + 256]
    pl.semaphore_wait(barrier, len(friends))

    x_in = ItemExchange(here, xs, r.x, r.xsend.at[0], r.xrecv.at[0], r.xlocal.at[0])
    dy_in = Exchange(here, dys, r.dy, r.esend.at[0], r.erecv.at[0], r.local.at[1])
    y_out = Exchange(here, r.dy, y, r.esend.at[1], r.erecv.at[1], r.local.at[2])
    dx_out = ItemExchange(here, r.x, dx, r.xsend.at[1], r.xrecv.at[1], r.xlocal.at[1])

    def gather(dst, n):
        return Gather(here, dst, r.gsend.at[n], r.grecv.at[n])

    g_q = [gather(r.wqkv.at[0, :, :, :, :, pl.ds(256 * w, 256)], 10 + w) for w in range(3)]
    g_q += [gather(r.wqkv.at[hq], hq) for hq in (1, 2)]
    g_o = gather(r.wo, 3)
    g_u = [
        (SplitGather if c in SPLIT_UP else Gather)(here, r.wup.at[c], r.gsend.at[4 + c], r.grecv.at[4 + c])
        for c in range(CHUNKS)
    ]
    g_d = [gather(r.wdn.at[c], 7 + c) for c in range(CHUNKS)]

    def reduce(kind, n, index, g, rc, place, count, credit, out):
        boxes = [getattr(r, box + kind).at[n] for box in ("ry", "rz", "rx", "tt")]
        args = (here, g, rc, place, count, credit, *boxes, out, r.rsend.at[index], r.rrecv.at[index])
        if kind == "d" and n in SPLIT_DOWN:
            return SplitReduce(r.rx0.at[n - 1], *args)
        return Reduce(*args)

    s_d = [
        reduce("d", c, 2 * c, r.gdn.at[c], r.rcd.at[c % 2], c, 3, r.credit_d, o_dn.at[c])
        for c in range(CHUNKS)
    ]
    s_u = [
        reduce("u", c, 2 * c + 1, r.wup.at[c], r.rcu.at[c % 2], c, 7, r.credit_u, o_up.at[c])
        for c in range(CHUNKS)
    ]
    narrow = [r.rcu.at[n % 2, :, :, :, pl.ds(0, D)] for n in range(2)]
    s_o = reduce("q", 3, 6, r.wo, narrow[1], 3, 7, r.credit_u, o_o)
    s_q = [
        reduce("q", c, 7 + c, layer.qkv_grad(c), narrow[c % 2], 4 + c, 7, r.credit_u, o_q.at[c])
        for c in range(2)
    ]
    for w in range(3):
        third = pl.ds(256 * w, 256)
        boxes = [r.ryq.at[2, :, :, third], r.rzq.at[2, :, :, third], r.rxq.at[2, :, third], r.ttq.at[2, :, :, third]]
        s_q.append(
            Reduce(
                here, r.wdn.at[2, :, :, :, pl.ds(0, 48), third], r.rcu.at[0, :, :, :, third],
                6 if w == 0 else None, 7, r.credit_u, *boxes, o_q.at[2, :, :, third],
                r.rsend.at[9 + w], r.rrecv.at[9 + w],
            )
        )
    sums = ReduceVectors(here, r.gv, r.gbox, r.wbox, r.gvw, r.wsend, r.wrecv)

    units = {"O": g_o, "o": s_o}
    for c in range(CHUNKS):
        units |= {f"U{c}": g_u[c], f"D{c}": g_d[c], f"d{c}": s_d[c], f"u{c}": s_u[c]}
    units |= dict(zip(("Q0q", "Q0k", "Q0v", "Q1", "Q2"), g_q))
    units |= dict(zip(("q0", "q1", "q2q", "q2k", "q2v"), s_q))

    def at(slot):
        for unit, name in TIMETABLE.get(slot, ()):
            getattr(units[unit], MOVES[name])()

    def slots(**names):
        return {
            index: (lambda slot=slot: at(slot)) for slot, index in names.items() if slot in TIMETABLE
        }

    at("start")
    x_in.start()
    at("more")

    rows = lax.broadcasted_iota(jnp.int32, (96, WINDOW), 0)
    cols = lax.broadcasted_iota(jnp.int32, (96, WINDOW), 1)
    chosen = jnp.where(cols - (here.i * 96 - window_start(here.i)) == rows, 1.0, 0.0).astype(bf)
    r.vbox[here.i] = jnp.concatenate(
        [nn(w_vec[...].astype(bf), chosen), jnp.zeros((VROWS - 12, WINDOW), f32)], 0
    ).astype(bf)
    table = Mail(here, r.vsend, r.vrecv)
    for k in range(1, OWNERS):
        own = r.vbox.at[here.i]
        table.go(own, own, k - 1, here.at_items(k))
    layer.start()
    loads[3].wait()
    r.wo[here.z, here.y, here.c] = r.x2[1, 1, :48, :].astype(bf)
    for q in range(4):
        loads[4 + q].wait()
        part = r.x2[2 + q // 2, q % 2, :48, :].astype(bf)
        for m in range(6):
            i, c = (6 * q + m) // 3, (6 * q + m) % 3

            def put(i=i, c=c, part=part[:, m * 128 : (m + 1) * 128]):
                r.wup[c, here.z, here.y, here.c, :, i * 128 : (i + 1) * 128] = part

            if c in SPLIT_UP:
                pl.when(here.x == i // 4)(put)
            else:
                put()
    for c in range(CHUNKS):
        loads[8 + c].wait()
        r.wdn[c, here.z, here.y, here.c] = r.yacc[c // 2, c % 2, :64, :].astype(bf)

    at("cast")
    for k in range(1, OWNERS):
        table.arrived(r.vbox.at[(here.i + OWNERS - k) % OWNERS], k - 1)
    r.vec[...] = jnp.zeros_like(r.vec)
    for n in range(OWNERS):
        start = window_start(n)
        r.vec[:, start : start + WINDOW] += r.vbox[n].astype(f32)
    layer.spread_biases()
    at("table")
    x_in.arrive(0)
    layer.norm_item(0)
    at("ln0")

    def other_item():
        x_in.arrive(1)
        layer.norm_item(1)

    in_parts = slots(**{f"s{n}{'pab'[j]}": 3 * n + j for n in range(6) for j in range(3)})
    for index, extra in ((2, dy_in.start), (8, other_item)):

        def both(before=in_parts.get(index, lambda: None), extra=extra):
            before()
            extra()

        in_parts[index] = both

    def part(n, _):
        layer.attend(n, in_parts)
        return 0

    lax.fori_loop(0, 6, part, 0)
    dy_in.arrive()
    at("dy")
    layer.middle(slots(**{f"m{k}": k for k in range(GROUPS)}))
    in_feed = {f"f{c}{j}": 10 * c + j for c in range(CHUNKS) for j in range(4)}
    in_feed |= {f"g{c}{n}": 10 * c + 4 + n for c in range(CHUNKS) for n in range(4)}
    in_feed = slots(**in_feed)
    for c in range(CHUNKS):

        def overwrite(c=c, before=in_feed.get(10 * c + 5, lambda: None)):
            before()
            g_u[c].drain()

        in_feed[10 * c + 5] = overwrite
    layer.feed(in_feed)
    dy_in.drain()
    layer.turn(y_out.order, y_out.put, slots(**{f"t{k}": k for k in range(GROUPS)}))
    g_o.drain()
    for c in range(CHUNKS):
        g_d[c].drain()
    layer.out_grads()
    at("gwo")
    in_back = {f"b{q}{k}": 10 * q + k for q in range(3) for k in range(4)}
    in_back |= {f"gq{q}": 10 * q + 5 for q in range(3)}
    in_back |= {f"on{q}{t}": 10 * q + 6 + t for q in range(3) for t in range(2)}
    in_back |= {f"fin{t}": 28 + t for t in range(2)}
    layer.attend_back(slots(**in_back), dx_out.order, dx_out.put)
    sums.first()
    y_out.arrive()
    for part in g_q + [x_in, y_out]:
        part.drain()
    table.left(r.vbox.at[0], *range(OWNERS - 1))
    at("tail0")
    sums.second()
    for part in s_d + s_u + [s_o]:
        part.drain()
    at("tail1")
    sums.third()
    store = pltpu.make_async_copy(r.gvw, gv, r.local.at[4])
    store.start()
    at("tail2")
    dx_out.arrive(0)
    dx_out.arrive(1)
    store.wait()
    for part in s_q + [sums, dx_out]:
        part.drain()


def step(x, dy, counts, masks, weights):
    scratch = [pltpu.VMEM(*spec) for spec in (LAYER_BUFFERS | COMM_BUFFERS).values()]
    scratch += [pltpu.SemaphoreType.DMA(shape) for shape in SEMS.values()]
    scratch += [pltpu.SemaphoreType.REGULAR] * 2
    return pl.pallas_call(
        step_kernel,
        out_shape=(
            jax.ShapeDtypeStruct(TOKENS, bf),
            jax.ShapeDtypeStruct(TOKENS, bf),
            jax.ShapeDtypeStruct((VROWS, WINDOW), f32),
            jax.ShapeDtypeStruct((CHUNKS, 2, 384, 128), bf),
            jax.ShapeDtypeStruct((CHUNKS, 2, 48, WIDE), bf),
            jax.ShapeDtypeStruct((2, 48, D), bf),
            jax.ShapeDtypeStruct((3, 2, 48, D), bf),
        ),
        in_specs=[ANY, ANY, SMEM, SMEM, ANY, ANY, ANY, ANY, VMEM],
        out_specs=[ANY] * 7,
        scratch_shapes=scratch,
        compiler_params=pltpu.CompilerParams(
            collective_id=1, has_side_effects=True, vmem_limit_bytes=63 * MIB + 512 * 1024
        ),
    )(x, dy, counts, masks, *weights)


def update_kernel(*refs):
    states = [refs[5 * n : 5 * n + 5] for n in range(3)]
    gv, *grads_in, y_in, dx_in = refs[15:22]
    y, dx = refs[22:24]
    news = [refs[24 + 5 * n : 29 + 5 * n] for n in range(3)]
    b_qkv, b_o, b_up, b_dn, g_dn, g_up, g_o, g_q, out, low, wide, s_in, s_out, s_grad, s_tok = refs[39:]
    boxes = (b_qkv, b_o, b_up, b_dn)
    load_y = pltpu.make_async_copy(y_in, out, s_tok.at[0])
    load_dx = pltpu.make_async_copy(dx_in, low, s_tok.at[1])
    store_dx = pltpu.make_async_copy(wide, dx, s_tok.at[2])
    store_y = pltpu.make_async_copy(out, y, s_tok.at[3])
    grad_loads = [
        pltpu.make_async_copy(src, dst, s_grad.at[n])
        for n, (src, dst) in enumerate(zip(grads_in, (g_dn, g_up, g_o, g_q)))
    ]
    parts = [(1, pl.ds(0, 96))]
    parts += [(2, pl.ds(48 * h, 48)) for h in range(2)]
    parts += [(0, pl.ds(48 * h, 48)) for h in range(2)]
    parts += [(3, pl.ds(128 * c, 128)) for c in range(CHUNKS)]

    def load(n):
        a, rows = parts[n]
        return [
            pltpu.make_async_copy(states[k][a].at[rows], boxes[a].at[k, rows], s_in.at[n, k]) for k in range(3)
        ]

    def store(n):
        a, rows = parts[n]
        return [
            pltpu.make_async_copy(boxes[a].at[k, rows], news[k][a].at[rows], s_out.at[n, k]) for k in range(3)
        ]

    def start(copies):
        for copy in copies:
            copy.start()

    def wait(copies):
        for copy in copies:
            copy.wait()

    start([grad_loads[2]] + load(0) + [grad_loads[1]] + load(1) + load(2))
    start([grad_loads[3], load_dx, load_y])

    def update(a, rows, cols, grad):
        box = boxes[a]
        new = adamw(
            box[0, rows, cols], box[1, rows, cols], box[2, rows, cols], grad.astype(f32), rates[a], decays[a]
        )
        for k in range(3):
            box[k, rows, cols] = new[k]

    for n, (a, rows) in enumerate(parts):
        if n + 3 < len(parts):
            if n + 3 == 5:
                start([grad_loads[0]])
            start(load(n + 3))
        if n in (0, 1, 3, 5):
            grad_loads[(2, 1, None, 3, None, 0)[n]].wait()
        wait(load(n))
        if a == 1:
            for h in range(2):
                update(1, slice(48 * h, 48 * h + 48), slice(0, D), g_o[h])
        elif a == 2:
            h = n - 1
            for c in range(CHUNKS):
                for i in range(OWNERS):
                    cols = slice((3 * i + c) * 128, (3 * i + c + 1) * 128)
                    update(2, slice(48 * h, 48 * h + 48), cols, g_up[c, h, :, i * 128 : (i + 1) * 128])
        elif a == 0:
            h = n - 3
            for hq in range(3):
                for w in range(3):
                    cols = slice(w * D + hq * 256, w * D + hq * 256 + 256)
                    update(0, slice(48 * h, 48 * h + 48), cols, g_q[hq, h, :, w * 256 : w * 256 + 256])
        else:
            c = n - 5
            for h in range(2):
                update(
                    3,
                    slice(128 * c, 128 * c + 128),
                    slice(384 * h, 384 * h + 384),
                    g_dn[c, h].astype(f32).T,
                )
        start(store(n))
        if n == 2:
            load_dx.wait()
            wide[...] = low[...].astype(f32)
            load_y.wait()
            start([store_dx, store_y])

    here = lax.axis_index("items")
    first = here * 96 - window_start(here)
    rows = lax.broadcasted_iota(jnp.int32, (WINDOW, 96), 0)
    cols = lax.broadcasted_iota(jnp.int32, (WINDOW, 96), 1)
    chosen = jnp.where(rows - first == cols, 1.0, 0.0)
    grad = jnp.dot(gv[...], chosen, preferred_element_type=f32, precision=lax.Precision.HIGHEST)
    new = adamw(states[0][4][...], states[1][4][...], states[2][4][...], grad[:12], rates[4], decays[4])
    for k in range(3):
        news[k][4][...] = new[k]
    for n in range(len(parts)):
        wait(store(n))
    wait([store_dx, store_y])


def update(masters, firsts, seconds, gv, grads, y, dx):
    big = [ANY] * 4 + [VMEM]
    shapes = [jax.ShapeDtypeStruct(m.shape, f32) for m in masters]
    out = pl.pallas_call(
        update_kernel,
        out_shape=[jax.ShapeDtypeStruct(TOKENS, bf), jax.ShapeDtypeStruct(TOKENS, f32)] + shapes * 3,
        in_specs=big * 3 + [VMEM] + [ANY] * 6,
        out_specs=[ANY, ANY] + big * 3,
        scratch_shapes=[
            pltpu.VMEM((3, 96, 3 * D), f32),
            pltpu.VMEM((3, 96, D), f32),
            pltpu.VMEM((3, 96, FF), f32),
            pltpu.VMEM((3, 384, D), f32),
        ]
        + [pltpu.VMEM(g.shape, bf) for g in grads]
        + [
            pltpu.VMEM(TOKENS, bf),
            pltpu.VMEM(TOKENS, bf),
            pltpu.VMEM(TOKENS, f32),
            pltpu.SemaphoreType.DMA((8, 3)),
            pltpu.SemaphoreType.DMA((8, 3)),
            pltpu.SemaphoreType.DMA((4,)),
            pltpu.SemaphoreType.DMA((4,)),
        ],
        compiler_params=pltpu.CompilerParams(vmem_limit_bytes=63 * MIB),
    )(*masters, *firsts, *seconds, gv, *grads, y, dx)
    return out[0], out[1], [out[2 + 5 * k : 7 + 5 * k] for k in range(3)]


def plain_kernel(*refs):
    (xs, dys, counts, masks, w_qkv, w_o, w_up, w_dn, vecs, y, dx, gv, o_dn, o_up, o_o, o_q) = refs[:16]
    r = collections.namedtuple("Refs", list(LAYER_BUFFERS) + ["sem"])(*refs[16:])
    layer = Layer(r, Masks(counts, masks))
    loads = [(xs, r.x), (dys, r.dy), (w_qkv, r.wqkv), (w_o, r.wo), (w_up, r.wup), (w_dn, r.wdn), (vecs, r.vec)]

    def move(pairs):
        copies = [pltpu.make_async_copy(s, d, r.sem.at[n]) for n, (s, d) in enumerate(pairs)]
        for copy in copies:
            copy.start()
        for copy in copies:
            copy.wait()

    move(loads)
    layer.start()
    layer.spread_biases()
    for t in range(2):
        layer.norm_item(t)

    def part(n, _):
        layer.attend(n, {})
        return 0

    lax.fori_loop(0, 6, part, 0)
    layer.middle({})
    layer.feed({})
    move([(r.wup, o_up), (r.gdn, o_dn)])
    layer.turn(lambda k: k, lambda k, g: None, {})
    layer.out_grads()
    layer.attend_back({}, lambda k: k, lambda k, t: None)
    move(
        [(r.dy, y), (r.x, dx), (r.gv, gv), (r.wo, o_o)]
        + [(layer.qkv_grad(hq), o_q.at[hq]) for hq in range(3)]
    )


def plain_step(x, dy, counts, masks, weights):
    def swap(values):
        return lax.all_to_all(values, "blk", 0, 0, tiled=True)

    full = [lax.all_gather(w.astype(bf), "items", axis=0, tiled=True) for w in weights[:4]]
    vecs = lax.all_gather(weights[4].astype(bf), "items", axis=1, tiled=True).astype(f32)
    w_qkv = full[0].reshape(D, 3, 3, 256).transpose(2, 0, 1, 3).reshape(3, 4, 2, 2, 48, D)
    w_o = full[1].reshape(4, 2, 2, 48, D)
    w_up = full[2].reshape(D, OWNERS, CHUNKS, 128).transpose(2, 0, 1, 3).reshape(CHUNKS, 4, 2, 2, 48, WIDE)
    w_dn = full[3].reshape(OWNERS, CHUNKS, 128, D).transpose(1, 0, 2, 3).reshape(CHUNKS, 4, 2, 2, 64, D)
    vecs = jnp.pad(vecs, ((0, VROWS - vecs.shape[0]), (0, 0)))
    y, dx, gv, g_dn, g_up, g_o, g_q = pl.pallas_call(
        plain_kernel,
        out_shape=(
            jax.ShapeDtypeStruct(TOKENS, bf),
            jax.ShapeDtypeStruct(TOKENS, bf),
            jax.ShapeDtypeStruct((VROWS, D), f32),
            jax.ShapeDtypeStruct((CHUNKS, 4, 2, 2, 384, 128), bf),
            jax.ShapeDtypeStruct((CHUNKS, 4, 2, 2, 48, WIDE), bf),
            jax.ShapeDtypeStruct((4, 2, 2, 48, D), bf),
            jax.ShapeDtypeStruct((3, 4, 2, 2, 48, D), bf),
        ),
        in_specs=[ANY, ANY, SMEM, SMEM] + [ANY] * 5,
        out_specs=[ANY] * 7,
        scratch_shapes=[pltpu.VMEM(*spec) for spec in LAYER_BUFFERS.values()]
        + [pltpu.SemaphoreType.DMA((8,))],
        compiler_params=pltpu.CompilerParams(vmem_limit_bytes=63 * MIB),
    )(swap(x), swap(dy), counts, masks, w_qkv, w_o, w_up, w_dn, vecs)
    g_up = g_up.reshape(CHUNKS, D, OWNERS, 128).transpose(1, 2, 0, 3).reshape(D, FF)
    g_dn = g_dn.reshape(CHUNKS, OWNERS, D, 128).transpose(1, 0, 3, 2).reshape(FF, D)
    g_q = g_q.reshape(3, D, 3, 256).transpose(1, 2, 0, 3).reshape(D, 3 * D)

    def total(values, axis):
        share = lax.psum_scatter(values.astype(f32), "items", scatter_dimension=axis, tiled=True)
        return lax.psum(share, "blk")

    grads = [total(v, 0) for v in (g_q, g_o.reshape(D, D), g_up, g_dn)] + [total(gv[:12], 1)]
    return swap(y), swap(dx).astype(f32), grads


def body(block_input, block_cotangent, task_counts, group_mask, *states):
    masters, firsts, seconds = states[:5], states[5:10], states[10:]
    x = block_input.reshape(TOKENS)
    dy = block_cotangent.reshape(TOKENS)
    allowed = group_mask.transpose(1, 2, 0)
    if lax.axis_size("items") == OWNERS and lax.axis_size("blk") == GROUPS:
        y, dx, gv, *grads = step(x, dy, task_counts, allowed, masters)
        y, dx, new = update(masters, firsts, seconds, gv, grads, y, dx)
    else:
        y, dx, grads = plain_step(x, dy, task_counts, allowed, masters)
        parts = [
            adamw(masters[n], firsts[n], seconds[n], grads[n], rates[n], decays[n]) for n in range(5)
        ]
        new = [[part[k] for part in parts] for k in range(3)]
    return (y.reshape(block_input.shape), dx.reshape(block_input.shape), *new[0], *new[1], *new[2])


def solution(mesh):
    tokens = P("items", "blk", None, None)
    rows = P("items", None)
    state = (rows, rows, rows, rows, P(None, "items"))
    return jax.shard_map(
        body,
        mesh=mesh,
        in_specs=(tokens, tokens, P("items"), P("items", None, None)) + state * 3,
        out_specs=(tokens, tokens) + state * 3,
        check_vma=False,
    )
```

time: 1060 us -> 209 us (0.20)
  waiting for transfers between devices: 450 us -> 0 us
  Pallas kernels: 0 us -> 208 us
  local copies, waits for them, and re-layouts: 195 us -> 0 us
  matrix products: 175 us -> 0 us
  other arithmetic: 103 us -> 0 us
  starting transfers between devices: 75.5 us -> 0 us
  blocking collectives: 38.3 us -> 0 us
  between operations: 15.4 us -> 0.82 us
    pallas_call x0 -> x2, Pallas kernels: none -> 208 us  [the longest x1 195 us: step(): pl.pallas_call(step_kernel, out_shape=(jax.ShapeDtypeStruct(TOKENS, bf),...]
    dot_general x26 -> x0, matrix products: 175 us -> none  [the longest x2 17.7 us: attend_back(): jnp.einsum('ighd,ijhd->ihgj', grad_mixed, values, preferred_element_type=...]
    reduce_scatter x4 -> x0, waiting for transfers between devices: 172 us -> none  [the longest x1 172 us: body(): lax.psum_scatter(grad_qkv, 'items', scatter_dimension=0, tiled=True)]
    slice x15 -> x0, local copies, waits for them, and re-layouts: 131 us -> none  [the longest x4 90.5 us: body(): carried = carried + slot_grads[hop]]
    ppermute x6 -> x0, waiting for transfers between devices: 98.6 us -> none  [from_behind(): return lax.ppermute(block, axis, route)]
    ppermute x6 -> x0, starting transfers between devices: 74.8 us -> none  [from_behind(): return lax.ppermute(block, axis, route)]
    psum x1 -> x0, waiting for transfers between devices: 69.6 us -> none  [body(): lax.psum((shares[0], shares[1], shares[2], shares[3], shares[4]), 'blk')]
    all_gather x4 -> x0, waiting for transfers between devices: 60.9 us -> none  [the longest x1 30.8 us: body(): lax.all_gather(weight_qkv.astype(bf), 'items', axis=0, tiled=True)]
  transfers between devices with their start and end apart: 16 -> 0, of which waited for: 9 -> 0; matrix products, arithmetic and copies ran while one was open for 39% -> 0% of each run, Pallas kernels for 0% -> 0%
where the time goes in v1:
time: 209 us
  Pallas kernels  208 us (100%)
    pallas_call x1, Pallas kernels, step(): pl.pallas_call(step_kernel, out_shape=(jax.ShapeDtypeStruct(TOKENS, bf),...  195 us
    pallas_call x1, Pallas kernels, update(): pl.pallas_call(update_kernel, out_shape=[jax.ShapeDtypeStruct(TOKENS, bf)...  13.3 us

profile of v1, /device:TPU:0, one launch (start us, length us, event | category | flops | bytes accessed | tf_op | source)
XLA Modules:
  0.0 208.7 jit_solution(10594658537711285369)
XLA Ops:
  0.7 194.6 %shard_map.314 = (bf16[4,2,128,768]{3,2,1,0:T(8,128)(2,1)}, bf16[4,2,128,768]{3,2,1,0:T(8,128)(2,1)}, f32[16,256]{1,0:T(8,128)}, bf16[3,2,384,128]{3,2,1,0:T(8,1...) custom-call(bf16[4,2,128,768]{3,2,1,0:T(8,128)(2,1)} %bitcast.9, ...), custom_call_target="tpu_custom_call" | custom-call | tf_op jit(solution)/shard_map/pallas_call | solution.py:1166
  195.2 13.3 %shard_map.315 = (bf16[4,2,128,768]{3,2,1,0:T(8,128)(2,1)}, f32[4,2,128,768]{3,2,1,0:T(8,128)}, f32[96,2304]{1,0:T(8,128)}, f32[96,768]{1,0:T(8,128)}, f32[96,30...) custom-call(f32[96,2304]{1,0:T(8,128)} %refs_0_.1, ...), custom_call_target="tpu_custom_call" | custom-call | tf_op jit(solution)/shard_map/pallas_call | solution.py:1293

commit v2 on v1

--- a/solution.py
+++ b/solution.py
@@ -33,7 +33,6 @@
 f32 = jnp.float32
 MESH = pl.DeviceIdType.MESH
 ANY = pl.BlockSpec(memory_space=pl.ANY)
-VMEM = pl.BlockSpec(memory_space=pltpu.VMEM)
 SMEM = pl.BlockSpec(memory_space=pltpu.SMEM)
 TOKENS = (GROUPS, 2, GROUP, D)
 
@@ -639,11 +638,10 @@
         def _():
             self.own(t).start()
 
-    def start(self):
-        for t in range(2):
-            for k in range(3):
-                self.copy(k, t).start()
-            self.own(t).start()
+    def start(self, t):
+        for k in range(3):
+            self.copy(k, t).start()
+        self.own(t).start()
 
     def arrive(self, t):
         self.own(t).wait()
@@ -859,6 +857,7 @@
     gbox=((GROUPS, VROWS, D), f32),
     wbox=((OWNERS, VROWS, WINDOW), f32),
     gvw=((VROWS, WINDOW), f32),
+    wvec=((12, 96), f32),
     rx0=((2, 4, 2, 192, 128), bf),
 )
 for _kind, _n, _rows, _cols in INBOXES:
@@ -867,9 +866,9 @@
     COMM_BUFFERS["rx" + _kind] = ((_n, _rows, _cols), bf)
     COMM_BUFFERS["tt" + _kind] = ((_n, 2, _rows, _cols), bf)
 SEMS = dict(
-    load=(11,),
-    gsend=(13, SplitGather.slots),
-    grecv=(13, SplitGather.slots),
+    load=(12,),
+    gsend=(12, SplitGather.slots),
+    grecv=(12, SplitGather.slots),
     rsend=(12, SplitReduce.slots),
     rrecv=(12, SplitReduce.slots),
     xsend=(2, 6),
@@ -885,7 +884,6 @@
 )
 
 
-SPLIT_UP = (0, 1, 2)
 SPLIT_DOWN = (1, 2)
 MOVES = dict(
     a="first", l="second", xx="across", h="third", w="last",
@@ -970,16 +968,12 @@
     for q in range(3):
         rows = pl.ds(q * 128 + here.c * 64, 64)
         loads.append((w_dn.at[rows], r.yacc.at[q // 2, q % 2, small_dn, :]))
+    loads.append((w_vec, r.wvec))
     loads = [pltpu.make_async_copy(s, d, r.load.at[n]) for n, (s, d) in enumerate(loads)]
     for load in loads:
         load.start()
 
     layer = Layer(r, Masks(counts, masks))
-    for q in range(3):
-        loads[q].wait()
-        part = r.x2[q // 2, q % 2, :48, :].astype(bf)
-        for hq in range(3):
-            r.wqkv[hq, here.z, here.y, here.c, :, q * 256 : q * 256 + 256] = part[:, hq * 256 : hq * 256 + 256]
     pl.semaphore_wait(barrier, len(friends))
 
     x_in = ItemExchange(here, xs, r.x, r.xsend.at[0], r.xrecv.at[0], r.xlocal.at[0])
@@ -987,17 +981,21 @@
     y_out = Exchange(here, r.dy, y, r.esend.at[1], r.erecv.at[1], r.local.at[2])
     dx_out = ItemExchange(here, r.x, dx, r.xsend.at[1], r.xrecv.at[1], r.xlocal.at[1])
 
-    def gather(dst, n):
-        return Gather(here, dst, r.gsend.at[n], r.grecv.at[n])
-
-    g_q = [gather(r.wqkv.at[0, :, :, :, :, pl.ds(256 * w, 256)], 10 + w) for w in range(3)]
-    g_q += [gather(r.wqkv.at[hq], hq) for hq in (1, 2)]
-    g_o = gather(r.wo, 3)
-    g_u = [
-        (SplitGather if c in SPLIT_UP else Gather)(here, r.wup.at[c], r.gsend.at[4 + c], r.grecv.at[4 + c])
-        for c in range(CHUNKS)
-    ]
-    g_d = [gather(r.wdn.at[c], 7 + c) for c in range(CHUNKS)]
+    count = iter(range(12))
+
+    def gather(dst, parts, kind=Gather):
+        width = dst.shape[-1] // parts
+        units = []
+        for p in range(parts):
+            n = next(count)
+            part = dst.at[:, :, :, :, pl.ds(p * width, width)]
+            units.append(kind(here, part, r.gsend.at[n], r.grecv.at[n]))
+        return units
+
+    g_q = [gather(r.wqkv.at[hq], 1 if hq else 3) for hq in range(3)]
+    (g_o,) = gather(r.wo, 1)
+    g_u = [gather(r.wup.at[c], 1, SplitGather) for c in range(CHUNKS)]
+    g_d = [gather(r.wdn.at[c], 1) for c in range(CHUNKS)]
 
     def reduce(kind, n, index, g, rc, place, count, credit, out):
         boxes = [getattr(r, box + kind).at[n] for box in ("ry", "rz", "rx", "tt")]
@@ -1032,11 +1030,13 @@
         )
     sums = ReduceVectors(here, r.gv, r.gbox, r.wbox, r.gvw, r.wsend, r.wrecv)
 
-    units = {"O": g_o, "o": s_o}
+    units = {"O": g_o, "o": s_o, "q0": s_q[0], "q1": s_q[1]}
     for c in range(CHUNKS):
-        units |= {f"U{c}": g_u[c], f"D{c}": g_d[c], f"d{c}": s_d[c], f"u{c}": s_u[c]}
-    units |= dict(zip(("Q0q", "Q0k", "Q0v", "Q1", "Q2"), g_q))
-    units |= dict(zip(("q0", "q1", "q2q", "q2k", "q2v"), s_q))
+        units |= {f"d{c}": s_d[c], f"u{c}": s_u[c]}
+        for base, parts in (("Q", g_q[c]), ("U", g_u[c]), ("D", g_d[c])):
+            names = ("q", "k", "v") if len(parts) > 1 else ("",)
+            units |= {f"{base}{c}{name}": part for name, part in zip(names, parts)}
+    units |= {f"q2{name}": part for name, part in zip("qkv", s_q[2:])}
 
     def at(slot):
         for unit, name in TIMETABLE.get(slot, ()):
@@ -1047,15 +1047,21 @@
             index: (lambda slot=slot: at(slot)) for slot, index in names.items() if slot in TIMETABLE
         }
 
+    x_in.start(0)
+    for q in range(3):
+        loads[q].wait()
+        part = r.x2[q // 2, q % 2, :48, :].astype(bf)
+        for hq in range(3):
+            r.wqkv[hq, here.z, here.y, here.c, :, q * 256 : q * 256 + 256] = part[:, hq * 256 : hq * 256 + 256]
     at("start")
-    x_in.start()
     at("more")
 
     rows = lax.broadcasted_iota(jnp.int32, (96, WINDOW), 0)
     cols = lax.broadcasted_iota(jnp.int32, (96, WINDOW), 1)
     chosen = jnp.where(cols - (here.i * 96 - window_start(here.i)) == rows, 1.0, 0.0).astype(bf)
+    loads[11].wait()
     r.vbox[here.i] = jnp.concatenate(
-        [nn(w_vec[...].astype(bf), chosen), jnp.zeros((VROWS - 12, WINDOW), f32)], 0
+        [nn(r.wvec[...].astype(bf), chosen), jnp.zeros((VROWS - 12, WINDOW), f32)], 0
     ).astype(bf)
     table = Mail(here, r.vsend, r.vrecv)
     for k in range(1, OWNERS):
@@ -1070,13 +1076,10 @@
         for m in range(6):
             i, c = (6 * q + m) // 3, (6 * q + m) % 3
 
-            def put(i=i, c=c, part=part[:, m * 128 : (m + 1) * 128]):
+            @pl.when(here.x == i // 4)
+            def _(i=i, c=c, part=part[:, m * 128 : (m + 1) * 128]):
                 r.wup[c, here.z, here.y, here.c, :, i * 128 : (i + 1) * 128] = part
 
-            if c in SPLIT_UP:
-                pl.when(here.x == i // 4)(put)
-            else:
-                put()
     for c in range(CHUNKS):
         loads[8 + c].wait()
         r.wdn[c, here.z, here.y, here.c] = r.yacc[c // 2, c % 2, :64, :].astype(bf)
@@ -1091,6 +1094,7 @@
     layer.spread_biases()
     at("table")
     x_in.arrive(0)
+    x_in.start(1)
     layer.norm_item(0)
     at("ln0")
 
@@ -1122,15 +1126,16 @@
 
         def overwrite(c=c, before=in_feed.get(10 * c + 5, lambda: None)):
             before()
-            g_u[c].drain()
+            for part in g_u[c]:
+                part.drain()
 
         in_feed[10 * c + 5] = overwrite
     layer.feed(in_feed)
     dy_in.drain()
     layer.turn(y_out.order, y_out.put, slots(**{f"t{k}": k for k in range(GROUPS)}))
     g_o.drain()
-    for c in range(CHUNKS):
-        g_d[c].drain()
+    for part in g_d[0] + g_d[1] + g_d[2]:
+        part.drain()
     layer.out_grads()
     at("gwo")
     in_back = {f"b{q}{k}": 10 * q + k for q in range(3) for k in range(4)}
@@ -1140,7 +1145,7 @@
     layer.attend_back(slots(**in_back), dx_out.order, dx_out.put)
     sums.first()
     y_out.arrive()
-    for part in g_q + [x_in, y_out]:
+    for part in g_q[0] + g_q[1] + g_q[2] + [x_in, y_out]:
         part.drain()
     table.left(r.vbox.at[0], *range(OWNERS - 1))
     at("tail0")
@@ -1174,7 +1179,7 @@
             jax.ShapeDtypeStruct((2, 48, D), bf),
             jax.ShapeDtypeStruct((3, 2, 48, D), bf),
         ),
-        in_specs=[ANY, ANY, SMEM, SMEM, ANY, ANY, ANY, ANY, VMEM],
+        in_specs=[ANY, ANY, SMEM, SMEM] + [ANY] * 5,
         out_specs=[ANY] * 7,
         scratch_shapes=scratch,
         compiler_params=pltpu.CompilerParams(
@@ -1188,7 +1193,8 @@
     gv, *grads_in, y_in, dx_in = refs[15:22]
     y, dx = refs[22:24]
     news = [refs[24 + 5 * n : 29 + 5 * n] for n in range(3)]
-    b_qkv, b_o, b_up, b_dn, g_dn, g_up, g_o, g_q, out, low, wide, s_in, s_out, s_grad, s_tok = refs[39:]
+    b_qkv, b_o, b_up, b_dn, b_vec, g_dn, g_up, g_o, g_q, g_vec = refs[39:49]
+    out, low, wide, s_in, s_out, s_grad, s_tok, s_vec = refs[49:]
     boxes = (b_qkv, b_o, b_up, b_dn)
     load_y = pltpu.make_async_copy(y_in, out, s_tok.at[0])
     load_dx = pltpu.make_async_copy(dx_in, low, s_tok.at[1])
@@ -1198,6 +1204,9 @@
         pltpu.make_async_copy(src, dst, s_grad.at[n])
         for n, (src, dst) in enumerate(zip(grads_in, (g_dn, g_up, g_o, g_q)))
     ]
+    vec_loads = [pltpu.make_async_copy(states[k][4], b_vec.at[k], s_vec.at[k]) for k in range(3)]
+    vec_loads.append(pltpu.make_async_copy(gv, g_vec, s_vec.at[3]))
+    vec_stores = [pltpu.make_async_copy(b_vec.at[k], news[k][4], s_vec.at[4 + k]) for k in range(3)]
     parts = [(1, pl.ds(0, 96))]
     parts += [(2, pl.ds(48 * h, 48)) for h in range(2)]
     parts += [(0, pl.ds(48 * h, 48)) for h in range(2)]
@@ -1224,7 +1233,7 @@
             copy.wait()
 
     start([grad_loads[2]] + load(0) + [grad_loads[1]] + load(1) + load(2))
-    start([grad_loads[3], load_dx, load_y])
+    start(vec_loads + [grad_loads[3], load_dx, load_y])
 
     def update(a, rows, cols, grad):
         box = boxes[a]
@@ -1272,36 +1281,39 @@
             wide[...] = low[...].astype(f32)
             load_y.wait()
             start([store_dx, store_y])
-
-    here = lax.axis_index("items")
-    first = here * 96 - window_start(here)
-    rows = lax.broadcasted_iota(jnp.int32, (WINDOW, 96), 0)
-    cols = lax.broadcasted_iota(jnp.int32, (WINDOW, 96), 1)
-    chosen = jnp.where(rows - first == cols, 1.0, 0.0)
-    grad = jnp.dot(gv[...], chosen, preferred_element_type=f32, precision=lax.Precision.HIGHEST)
-    new = adamw(states[0][4][...], states[1][4][...], states[2][4][...], grad[:12], rates[4], decays[4])
-    for k in range(3):
-        news[k][4][...] = new[k]
+        if n == 4:
+            wait(vec_loads)
+            here = lax.axis_index("items")
+            first = here * 96 - window_start(here)
+            r_at = lax.broadcasted_iota(jnp.int32, (WINDOW, 96), 0)
+            c_at = lax.broadcasted_iota(jnp.int32, (WINDOW, 96), 1)
+            chosen = jnp.where(r_at - first == c_at, 1.0, 0.0)
+            grad = jnp.dot(g_vec[...], chosen, preferred_element_type=f32, precision=lax.Precision.HIGHEST)
+            new = adamw(b_vec[0], b_vec[1], b_vec[2], grad[:12], rates[4], decays[4])
+            for k in range(3):
+                b_vec[k] = new[k]
+            start(vec_stores)
+
     for n in range(len(parts)):
         wait(store(n))
-    wait([store_dx, store_y])
+    wait([store_dx, store_y] + vec_stores)
 
 
 def update(masters, firsts, seconds, gv, grads, y, dx):
-    big = [ANY] * 4 + [VMEM]
     shapes = [jax.ShapeDtypeStruct(m.shape, f32) for m in masters]
     out = pl.pallas_call(
         update_kernel,
         out_shape=[jax.ShapeDtypeStruct(TOKENS, bf), jax.ShapeDtypeStruct(TOKENS, f32)] + shapes * 3,
-        in_specs=big * 3 + [VMEM] + [ANY] * 6,
-        out_specs=[ANY, ANY] + big * 3,
+        in_specs=[ANY] * 22,
+        out_specs=[ANY] * 17,
         scratch_shapes=[
             pltpu.VMEM((3, 96, 3 * D), f32),
             pltpu.VMEM((3, 96, D), f32),
             pltpu.VMEM((3, 96, FF), f32),
             pltpu.VMEM((3, 384, D), f32),
+            pltpu.VMEM((3, 12, 96), f32),
         ]
-        + [pltpu.VMEM(g.shape, bf) for g in grads]
+        + [pltpu.VMEM(g.shape, g.dtype) for g in (*grads, gv)]
         + [
             pltpu.VMEM(TOKENS, bf),
             pltpu.VMEM(TOKENS, bf),
@@ -1310,6 +1322,7 @@
             pltpu.SemaphoreType.DMA((8, 3)),
             pltpu.SemaphoreType.DMA((4,)),
             pltpu.SemaphoreType.DMA((4,)),
+            pltpu.SemaphoreType.DMA((7,)),
         ],
         compiler_params=pltpu.CompilerParams(vmem_limit_bytes=63 * MIB),
     )(*masters, *firsts, *seconds, gv, *grads, y, dx)

time: 209 us -> 208 us (level)
  no operation moved by 1% of the time
where the time goes in v2:
time: 208 us; the launch traced here: 207 us
  Pallas kernels  206 us (99%)
    pallas_call x1, Pallas kernels, step(): pl.pallas_call(step_kernel, out_shape=(jax.ShapeDtypeStruct(TOKENS, bf),...  195 us
    pallas_call x1, Pallas kernels, update(): pl.pallas_call(update_kernel, out_shape=[jax.ShapeDtypeStruct(TOKENS, bf)...  12 us

profile of v2, /device:TPU:0, one launch (start us, length us, event | category | flops | bytes accessed | tf_op | source)
XLA Modules:
  0.0 207.3 jit_solution(16150647138713550790)
XLA Ops:
  0.7 194.5 %shard_map.314 = (bf16[4,2,128,768]{3,2,1,0:T(8,128)(2,1)}, bf16[4,2,128,768]{3,2,1,0:T(8,128)(2,1)}, f32[16,256]{1,0:T(8,128)}, bf16[3,2,384,128]{3,2,1,0:T(8,1...) custom-call(bf16[4,2,128,768]{3,2,1,0:T(8,128)(2,1)} %bitcast.9, ...), custom_call_target="tpu_custom_call" | custom-call | tf_op jit(solution)/shard_map/pallas_call | solution.py:1171
  195.2 12.0 %shard_map.315 = (bf16[4,2,128,768]{3,2,1,0:T(8,128)(2,1)}, f32[4,2,128,768]{3,2,1,0:T(8,128)}, f32[96,2304]{1,0:T(8,128)}, f32[96,768]{1,0:T(8,128)}, f32[96,30...) custom-call(f32[96,2304]{1,0:T(8,128)} %refs_0_.1, ...), custom_call_target="tpu_custom_call" | custom-call | tf_op jit(solution)/shard_map/pallas_call | solution.py:1304

commit v3 on v2

--- a/solution.py
+++ b/solution.py
@@ -100,9 +100,10 @@
     return jnp.concatenate([jnp.where(low, pair, zero), jnp.where(low, zero, pair)], 0)
 
 
-def run_hooks(hooks, index):
+def run_hooks(hooks, index, *digits, base=10):
     for at, hook in hooks.items():
-        pl.when(index == at)(hook)
+        if not digits or at % base in digits:
+            pl.when(index == at)(hook)
 
 
 def up_block(c, i):
@@ -220,7 +221,7 @@
         a1 = r.a2[:, t].reshape(GROUPS * GROUP, D)
         p = nn(a1, r.wqkv[hq].reshape(D, D)) + self.qkv_bias(hq)
         r.qkv[:, t, :, pl.ds(pl.multiple_of(hq * D, 128), D)] = p.astype(bf).reshape(GROUPS, GROUP, D)
-        run_hooks(hooks, 3 * part)
+        run_hooks(hooks, 3 * part, 0, base=3)
 
         def step(hp, _):
             lanes = [self.lanes(hq, hp, w) for w in range(3)]
@@ -237,7 +238,7 @@
                 p = (e * (1.0 / total)).astype(bf)
                 r.stats[6 * t + 2 * hq + hp, g : g + 1, :] = top + jnp.log(total)
                 r.o[g, t, :, out] = self.own_heads(nn(v2[:, :n], p))
-            run_hooks(hooks, 3 * part + 1 + hp)
+            run_hooks(hooks, 3 * part + 1 + hp, 1, 2, base=3)
             return 0
 
         lax.fori_loop(0, 2, step, 0)
@@ -288,7 +289,7 @@
         def chunk(c, _):
             def step(j, _):
                 column(c, j)
-                run_hooks(hooks, 10 * c + j)
+                run_hooks(hooks, 10 * c + j, 0, 1, 2, 3)
                 return 0
 
             def down_grad(h, _):
@@ -317,7 +318,7 @@
             lax.fori_loop(0, 4, step, 0)
             for n, act in enumerate((down_grad, up_back, up_grad, down)):
                 lax.fori_loop(0, 2, act, 0)
-                run_hooks(hooks, 10 * c + 4 + n)
+                run_hooks(hooks, 10 * c + 4 + n, 4 + n)
             return 0
 
         lax.fori_loop(0, CHUNKS, chunk, 0)
@@ -397,21 +398,21 @@
             def item(t, _):
                 def step(hp, _):
                     pair(hq, t, hp)
-                    run_hooks(hooks, 10 * hq + 2 * t + hp)
+                    run_hooks(hooks, 10 * hq + 2 * t + hp, 0, 1, 2, 3)
                     return 0
 
                 lax.fori_loop(0, 2, step, 0)
                 pl.when(t == 1)(lambda: grads(hq, cols))
-                run_hooks(hooks, 10 * hq + 4 + t)
+                run_hooks(hooks, 10 * hq + 4 + t, 4, 5)
                 rows = r.qkv[:, t, :, cols].reshape(512, D)
                 back = nt(rows, r.wqkv[hq].reshape(D, D))
                 r.yacc[:, t] += back.reshape(GROUPS, GROUP, D)
-                run_hooks(hooks, 10 * hq + 6 + t)
+                run_hooks(hooks, 10 * hq + 6 + t, 6, 7)
 
                 @pl.when(hq == 2)
                 def _():
                     lax.fori_loop(0, GROUPS, lambda k, _: finish(t, k), 0)
-                    run_hooks(hooks, 10 * hq + 8 + t)
+                    run_hooks(hooks, 10 * hq + 8 + t, 8, 9)
 
                 return 0
 

time: 208 us -> 205 us (0.986)
    pallas_call x1, Pallas kernels: 195 us -> 192 us  [step(): pl.pallas_call(step_kernel, out_shape=(jax.ShapeDtypeStruct(TOKENS, bf),...]
where the time goes in v3:
time: 205 us
  Pallas kernels  204 us (100%)
    pallas_call x1, Pallas kernels, step(): pl.pallas_call(step_kernel, out_shape=(jax.ShapeDtypeStruct(TOKENS, bf),...  192 us
    pallas_call x1, Pallas kernels, update(): pl.pallas_call(update_kernel, out_shape=[jax.ShapeDtypeStruct(TOKENS, bf)...  12 us

profile of v3, /device:TPU:0, one launch (start us, length us, event | category | flops | bytes accessed | tf_op | source)
XLA Modules:
  0.0 204.6 jit_solution(9329697432101970095)
XLA Ops:
  0.7 191.8 %shard_map.314 = (bf16[4,2,128,768]{3,2,1,0:T(8,128)(2,1)}, bf16[4,2,128,768]{3,2,1,0:T(8,128)(2,1)}, f32[16,256]{1,0:T(8,128)}, bf16[3,2,384,128]{3,2,1,0:T(8,1...) custom-call(bf16[4,2,128,768]{3,2,1,0:T(8,128)(2,1)} %bitcast.9, ...), custom_call_target="tpu_custom_call" | custom-call | tf_op jit(solution)/shard_map/pallas_call | solution.py:1172
  192.5 12.0 %shard_map.315 = (bf16[4,2,128,768]{3,2,1,0:T(8,128)(2,1)}, f32[4,2,128,768]{3,2,1,0:T(8,128)}, f32[96,2304]{1,0:T(8,128)}, f32[96,768]{1,0:T(8,128)}, f32[96,30...) custom-call(f32[96,2304]{1,0:T(8,128)} %refs_0_.1, ...), custom_call_target="tpu_custom_call" | custom-call | tf_op jit(solution)/shard_map/pallas_call | solution.py:1305
